TPU v7x, 256 devices: a whole 4x4x8 slice. The times are simulated.
256 devices in a mesh: cam: 32 (over z, y), pt: 8 (over x, core).
Axes of the slice: x: 4, y: 4, z: 8, core: 2. Of those that a mesh axis runs over, the one named last changes fastest.
Arguments:
- jacobian_cam: float32 [4, 18, 131072], P(None, None, ('cam', 'pt')), may hold values from -2 to 2
- jacobian_pt: float32 [4, 6, 131072], P(None, None, ('cam', 'pt'))
- residuals: float32 [4, 2, 131072], P(None, None, ('cam', 'pt')), may hold values from -8 to 8
- point_inverse: float32 [9, 131072], P(None, ('cam', 'pt')), as said below
- obs_camera: int32 [4, 131072], P(None, ('cam', 'pt')), may hold values from 0 to 32767, as said below
- pair_slot: int32 [4, 4, 131072], P(None, None, ('cam', 'pt')), may hold values from 0 to 12, as said below
- observation_used: int32 [4, 131072], P(None, ('cam', 'pt')), may hold values from 0 to 1, as said below
- pattern: int32 [12, 32768], P(None, ('cam', 'pt')), may hold values from 0 to 32767, as said below
Outputs:
- camera_step: float32 [9, 32768], P(None, ('cam', 'pt'))
- cam_residual: float32 [9, 32768], P(None, ('cam', 'pt'))
- point_step: float32 [3, 131072], P(None, ('cam', 'pt'))
Inputs may be any that keep to these rules, and one draw needn't show every extreme that they name: `obs_camera`: the 4 cameras of a point are distinct and lie within 12 places of one another in the order behind pattern. `pair_slot`: entry [a, b, j] is the place k with pattern[k, obs_camera[a, j]] = obs_camera[b, j], and 12 where a equals b. `observation_used`: among the live observations of the points of one device, at most 16 name cameras of one device's share; some pair of devices reaches it. `pattern`: column i lists 12 distinct cameras other than i; camera i is coupled to j exactly when j is coupled to i. `point_inverse`: the inverse of the identity plus the sum over the point's live observations of Jp^T Jp.
All inputs are finite; a program needn't handle non-finite values.
Results may differ from a plain program's by a relative error of at most 0.0003.
Values sent between devices are 32-bit elements; how exact they have to be, the bound alone decides.
No kernel may reach another device: no remote copies, remote signals or barrier semaphores. Data moves between devices by JAX's collectives and lax.ppermute only.
A program may use at most 128 MiB of HBM per device.

v0:
```python
import jax
import jax.numpy as jnp
from jax import lax
from jax.sharding import PartitionSpec as P

TRACK = 4
NBR = 12
ITERS = 4


DAMPING = 1.0


def point_terms(jacobian_cam, jacobian_pt, residuals, point_inverse, observation_used):
    npts = jacobian_cam.shape[-1]
    observation_active = observation_used.astype(jnp.float32)
    camera_jacobian_rows = jacobian_cam.reshape(TRACK, 2, 9, npts)
    point_jacobian_rows = jacobian_pt.reshape(TRACK, 2, 3, npts)
    inverse_blocks = point_inverse.reshape(3, 3, npts)
    camera_point_coupling = (
        jnp.sum(
            camera_jacobian_rows[:, :, :, None, :] * point_jacobian_rows[:, :, None, :, :], axis=1
        )
        * observation_active[:, None, None, :]
    )
    points_removed = jnp.sum(
        camera_point_coupling[:, :, :, None, :] * inverse_blocks[None, None, :, :, :], axis=2
    )
    point_gradient = -jnp.sum(
        observation_active[:, None, :]
        * jnp.sum(point_jacobian_rows * residuals[:, :, None, :], axis=1),
        axis=0,
    )
    camera_gradient = -observation_active[:, None, :] * jnp.sum(
        camera_jacobian_rows * residuals[:, :, None, :], axis=1
    )
    return (
        camera_jacobian_rows,
        camera_point_coupling,
        points_removed,
        point_gradient,
        camera_gradient,
        observation_active,
        inverse_blocks,
    )


def pair_block(square_root, partner, normal_terms):
    (
        camera_jacobian_rows,
        camera_point_coupling,
        points_removed,
        point_gradient,
        camera_gradient,
        observation_active,
        inverse_blocks,
    ) = normal_terms
    npts = camera_jacobian_rows.shape[-1]
    cross = -jnp.sum(
        points_removed[square_root][:, None, :, :] * camera_point_coupling[partner][None, :, :, :],
        axis=2,
    )
    if square_root == partner:
        gram_matrix = (
            jnp.sum(
                camera_jacobian_rows[square_root][:, :, None, :]
                * camera_jacobian_rows[square_root][:, None, :, :],
                axis=0,
            )
            * observation_active[square_root]
        )
        block = gram_matrix + cross
        right = camera_gradient[square_root] - jnp.sum(
            points_removed[square_root] * point_gradient[None, :, :], axis=1
        )
    else:
        block = cross
        right = jnp.zeros((9, npts), jnp.float32)
    return jnp.concatenate([block.reshape(81, npts), right], axis=0)


def factor_blocks(matrix):
    lower = {}
    for row_idx in range(9):
        for col_idx in range(row_idx + 1):
            accum = matrix[row_idx, col_idx]
            for inner_idx in range(col_idx):
                accum = accum - lower[row_idx, inner_idx] * lower[col_idx, inner_idx]
            if row_idx == col_idx:
                lower[row_idx, row_idx] = jnp.sqrt(accum)
            else:
                lower[row_idx, col_idx] = accum / lower[col_idx, col_idx]
    return lower


def solve_blocks(lower, vector):
    forward = []
    for row_idx in range(9):
        accum = vector[row_idx]
        for inner_idx in range(row_idx):
            accum = accum - lower[row_idx, inner_idx] * forward[inner_idx]
        forward.append(accum / lower[row_idx, row_idx])
    backward = [None] * 9
    for row_idx in reversed(range(9)):
        accum = forward[row_idx]
        for inner_idx in range(row_idx + 1, 9):
            accum = accum - lower[inner_idx, row_idx] * backward[inner_idx]
        backward[row_idx] = accum / lower[row_idx, row_idx]
    return jnp.stack(backward)


def apply_schur(blocks, pattern, direction):
    count = direction.shape[1]
    whole = lax.all_gather(direction, ("cam", "pt"), axis=1, tiled=True)
    taken = whole[:, pattern]
    stacked = jnp.concatenate([taken, direction[:, None, :]], axis=1)
    return jnp.einsum(
        "rckn,ckn->rn",
        blocks.reshape(9, 9, NBR + 1, count),
        stacked,
        precision=lax.Precision.HIGHEST,
    )


def energy_sum(remainder, precond):
    return lax.psum(jnp.sum(remainder * precond), ("cam", "pt"))


def per_device(
    jacobian_cam,
    jacobian_pt,
    residuals,
    point_inverse,
    obs_camera,
    pair_slot,
    observation_used,
    pattern,
):
    n_cam = lax.axis_size("cam")
    n_pt = lax.axis_size("pt")
    devices = n_cam * n_pt
    npts = obs_camera.shape[1]
    cam_dev = pattern.shape[1]
    obs_cap = 8 * npts // devices
    row_cap = TRACK * obs_cap
    total_slots = devices * row_cap
    normal_terms = point_terms(
        jacobian_cam, jacobian_pt, residuals, point_inverse, observation_used
    )
    owner_dev = obs_camera // cam_dev
    within = obs_camera % cam_dev
    keyed = jnp.where(observation_used > 0, owner_dev, devices).reshape(-1)
    total = keyed.shape[0]
    order = jnp.argsort(keyed * total + jnp.arange(total, dtype=jnp.int32))
    sorted_keys = keyed[order]
    starts = jnp.searchsorted(sorted_keys, sorted_keys, side="left")
    rank = (
        jnp.zeros((total,), jnp.int32)
        .at[order]
        .set(jnp.arange(total, dtype=jnp.int32) - starts)
        .reshape(TRACK, npts)
    )
    sentinel = (NBR + 1) * n_pt * cam_dev
    value_parts = []
    where_parts = []
    label_parts = []
    for square_root in range(TRACK):
        for partner in range(TRACK):
            value_parts.append(pair_block(square_root, partner, normal_terms))
            where_parts.append(
                jnp.where(
                    observation_used[square_root] > 0,
                    owner_dev[square_root] * row_cap + TRACK * rank[square_root] + partner,
                    total_slots,
                )
            )
            label_parts.append(pair_slot[square_root, partner] * cam_dev + within[square_root])
    values_all = jnp.concatenate(value_parts, axis=1)
    where_all = jnp.concatenate(where_parts, axis=0)
    labels_all = jnp.concatenate(label_parts, axis=0)
    outgoing = (
        jnp.zeros((90, total_slots), jnp.float32).at[:, where_all].set(values_all, mode="drop")
    )
    out_labels = (
        jnp.full((total_slots,), sentinel, jnp.int32).at[where_all].set(labels_all, mode="drop")
    )
    outgoing = outgoing.reshape(90, n_cam, n_pt, row_cap)
    out_labels = out_labels.reshape(1, n_cam, n_pt, row_cap)
    arrived, arrived_labels = (
        lax.all_to_all(outgoing, "cam", split_axis=1, concat_axis=1, tiled=True),
        lax.all_to_all(out_labels, "cam", split_axis=1, concat_axis=1, tiled=True),
    )
    group_idx = jnp.arange(n_pt, dtype=jnp.int32)[None, None, :, None]
    cell_index = jnp.where(
        arrived_labels < sentinel,
        arrived_labels // cam_dev * (n_pt * cam_dev)
        + group_idx * cam_dev
        + arrived_labels % cam_dev,
        sentinel,
    )
    buffer = jnp.zeros((90, (NBR + 1) * n_pt * cam_dev), jnp.float32)
    buffer = buffer.at[:, cell_index.reshape(-1)].add(arrived.reshape(90, -1), mode="drop")
    cells = lax.psum_scatter(
        buffer.reshape(90, NBR + 1, n_pt * cam_dev), "pt", scatter_dimension=2, tiled=True
    )
    identity = jnp.eye(9, dtype=jnp.float32).reshape(81)
    blocks = cells[:81].at[:, NBR, :].add(DAMPING * identity[:, None])
    gradient = cells[81:, NBR, :]
    lower = factor_blocks(blocks[:, NBR, :].reshape(9, 9, cam_dev))
    solution = jnp.zeros_like(gradient)
    remainder = gradient
    precond = solve_blocks(lower, remainder)
    direction = precond
    energy_now = energy_sum(remainder, precond)
    for step_idx in range(ITERS):
        image = apply_schur(blocks, pattern, direction)
        alpha = energy_now / lax.psum(jnp.sum(direction * image), ("cam", "pt"))
        solution = solution + alpha * direction
        remainder = remainder - alpha * image
        precond = solve_blocks(lower, remainder)
        energy_next = energy_sum(remainder, precond)
        direction = precond + energy_next / energy_now * direction
        energy_now = energy_next
    whole_step = lax.all_gather(solution, ("cam", "pt"), axis=1, tiled=True)
    (
        camera_jacobian_rows,
        camera_point_coupling,
        points_removed,
        point_gradient,
        camera_gradient,
        observation_active,
        inverse_blocks,
    ) = normal_terms
    reduced = point_gradient
    for square_root in range(TRACK):
        seen = whole_step[:, obs_camera[square_root]]
        reduced = reduced - jnp.sum(camera_point_coupling[square_root] * seen[:, None, :], axis=0)
    point_step = jnp.sum(inverse_blocks * reduced[None, :, :], axis=1)
    return (solution, remainder, point_step)


def solution(mesh):
    return jax.shard_map(
        per_device,
        mesh=mesh,
        in_specs=(
            P(None, None, ("cam", "pt")),
            P(None, None, ("cam", "pt")),
            P(None, None, ("cam", "pt")),
            P(None, ("cam", "pt")),
            P(None, ("cam", "pt")),
            P(None, None, ("cam", "pt")),
            P(None, ("cam", "pt")),
            P(None, ("cam", "pt")),
        ),
        out_specs=(P(None, ("cam", "pt")), P(None, ("cam", "pt")), P(None, ("cam", "pt"))),
        check_vma=False,
    )
```

profile of v0, /device:TPU:1, one launch (start us, length us, event | category | flops | bytes accessed | tf_op | source)
XLA Modules:
  0.0 1807.6 jit_solution(9118856703704386746)
XLA Ops:
  8.9 5.0 sort.17
  14.0 11.8 gather_fusion.1
  25.8 142.4 %while.26 = (s32[]{:T(128)}, u32[2048]{0:T(1024)S(1)}, u32[2048]{0:T(1024)S(1)}, s32[2048]{0:T(1024)S(1)}, s32[]{:T(128)}, /*index=5*/s32[]{:T(128)}, s32[]{}) while((s32[]{:T(128)}, u32[2048]{0:T(1024)S(1)}, u32[2048]{0:T(1024)S(1)}, s32[2048]{0:T(1024)S(1)}, s32[]{:T(128)}, /*index=5*/s32[]{:T(128)}, s32[]{}) %tuple.365), condition=%wide.region_2.0_spmd.clone, body=%wide.region_1.0_spmd.clone.sunk | while | flops 38916 | bytes 135269 | solution.py:156
  25.9 11.8 gather_fusion
  37.7 11.8 gather_fusion
  49.6 11.8 gather_fusion
  61.5 11.8 gather_fusion
  73.3 11.8 gather_fusion
  85.2 11.8 gather_fusion
  97.1 11.8 gather_fusion
  108.9 11.8 gather_fusion
  120.8 11.8 gather_fusion
  132.7 11.8 gather_fusion
  144.5 11.8 gather_fusion
  156.4 11.8 gather_fusion
  168.3 8.0 scatter_custom_fusion
  176.9 30.5 %scatter_custom_fusion.1 = s32[16384]{0:T(1024)S(1)} fusion(s32[8192]{0:T(1024)S(1)} %bitcast.770, s32[8192]{0:T(1024)S(1)} %constant_dynamic-update-slice_fusion.53, s32[]{:T(128)} %constant.125.clone.1), kind=kCustom, calls=%fused_computation.170 | custom fusion | bytes 65540 | tf_op jit(solution)/shard_map/scatter | solution.py:185
  208.2 12.6 all-to-all-start
  230.8 8.6 multiply_reduce_fusion.4
  240.1 1.0 neg.150
  241.8 1.0 neg.148
  243.5 1.0 neg.156
  245.2 1.0 neg.140
  254.5 1.2 pad_dynamic-update-slice_fusion.11
  255.7 1.0 pad_dynamic-update-slice_fusion.10
  258.6 1.0 multiply_add_fusion.2
  262.4 0.9 multiply_add_fusion.1
  263.8 3.4 copy.769
  267.3 24.5 %scatter_custom_fusion.2 = f32[90,16384]{0,1:T(8,128)} fusion(s32[8192]{0:T(1024)} %bitcast.771, f32[8192,90]{1,0:T(8,128)} %copy.769, f32[]{:T(128)} %constant.124.clone.1), kind=kCustom, calls=%fused_computation.18 | custom fusion | bytes 5898752 | tf_op jit(solution)/shard_map/scatter | solution.py:182
  291.8 9.3 all-to-all-start.1
  301.7 1.6 reduce.28
  303.7 188.5 %all-to-all-done.1 = f32[90,32,8,64]{0,3,2,1:T(8,128)} async-done(((f32[90,32,8,64]{0,3,2,1:T(8,128)}), f32[90,32,8,64]{0,3,2,1:T(8,128)}, u32[]{:S(2)}, u32[]{:S(2)}) %all-to-all-start.1) | async-done | bytes 5898272 | tf_op jit(solution)/shard_map/all_to_all | solution.py:190
  492.3 90.8 %scatter_custom_fusion.3 = f32[90,13312]{0,1:T(8,128)} fusion(s32[16384]{0:T(1024)S(1)} %bitcast.753, f32[16384,90]{1,0:T(8,128)} %bitcast.62, f32[]{:T(128)} %constant.124.clone.1), kind=kCustom, calls=%fused_computation.20 | custom fusion | flops 1474560 | bytes 4792832 | tf_op jit(solution)/shard_map/scatter-add | solution.py:202
  583.1 8.1 copy.816
  591.3 41.4 %reduce-scatter.2.cloned.1.call-done = f32[90,13,128]{2,1,0:T(8,128)} async-done(((f32[90,13,1024]{2,1,0:T(8,128)}), f32[90,13,128]{2,1,0:T(8,128)}) %reduce-scatter.2.cloned.1.call-update) | async-done | bytes 599056 | tf_op jit(solution)/shard_map/reduce_scatter | solution.py:203
  632.7 1.2 fusion.235
  635.7 1.2 stack.110
  637.8 1.1 slice.795
  638.9 2.4 scatter-add.13
  643.8 99.7 %all-gather.6.cloned.1.call-done = f32[9,32768]{1,0:T(8,128)} async-done(((f32[9,128]{1,0:T(8,128)}), f32[9,32768]{1,0:T(8,128)}) %all-gather.6.cloned.1.call-update) | async-done | bytes 1179664 | tf_op jit(solution)/shard_map/all_gather | solution.py:114
  743.5 9.8 copy.771
  753.3 8.4 gather_fusion.2
  762.7 77.1 %all-reduce.12 = (f32[]{:T(128)}, f32[]{:T(128)}) all-reduce(f32[]{:T(128)} %get-tuple-element.133, f32[]{:T(128)} %get-tuple-element.132), channel_id=1, replica_groups=mesh['cam'=32,'pt'=8] {'cam','pt'}, use_global_device_ids=true, to_apply=%region_38.39 | all-reduce | flops 2 | bytes 16 | tf_op jit(solution)/shard_map/psum | solution.py:126
  842.1 72.6 %psum.58 = f32[]{:T(128)} all-reduce(f32[]{:T(128)} %multiply_reduce_fusion.40), channel_id=1, replica_groups=mesh['cam'=32,'pt'=8] {'cam','pt'}, use_global_device_ids=true, to_apply=%region_42.43 | all-reduce | flops 1 | bytes 8 | tf_op jit(solution)/shard_map/psum | solution.py:126
  917.1 100.0 %all-gather.8.cloned.1.call-done = f32[9,32768]{1,0:T(8,128)} async-done(((f32[9,128]{1,0:T(8,128)}), f32[9,32768]{1,0:T(8,128)}) %all-gather.8.cloned.1.call-update) | async-done | bytes 1179664 | tf_op jit(solution)/shard_map/all_gather | solution.py:114
  1017.1 9.8 copy.774
  1026.9 8.4 gather_fusion.3
  1036.3 77.0 %psum.59 = f32[]{:T(128)} all-reduce(f32[]{:T(128)} %fusion.20), channel_id=1, replica_groups=mesh['cam'=32,'pt'=8] {'cam','pt'}, use_global_device_ids=true, to_apply=%region_44.45 | all-reduce | flops 1 | bytes 8 | tf_op jit(solution)/shard_map/psum | solution.py:217
  1115.5 72.6 %psum.60 = f32[]{:T(128)} all-reduce(f32[]{:T(128)} %multiply_reduce_fusion.39), channel_id=1, replica_groups=mesh['cam'=32,'pt'=8] {'cam','pt'}, use_global_device_ids=true, to_apply=%region_46.47 | all-reduce | flops 1 | bytes 8 | tf_op jit(solution)/shard_map/psum | solution.py:126
  1190.3 100.3 %all-gather.10.cloned.1.call-done = f32[9,32768]{1,0:T(8,128)} async-done(((f32[9,128]{1,0:T(8,128)}), f32[9,32768]{1,0:T(8,128)}) %all-gather.10.cloned.1.call-update) | async-done | bytes 1179664 | tf_op jit(solution)/shard_map/all_gather | solution.py:114
  1290.6 9.8 copy.776
  1300.4 8.4 gather_fusion.4
  1309.8 77.0 %psum.61 = f32[]{:T(128)} all-reduce(f32[]{:T(128)} %fusion.18), channel_id=1, replica_groups=mesh['cam'=32,'pt'=8] {'cam','pt'}, use_global_device_ids=true, to_apply=%region_48.49 | all-reduce | flops 1 | bytes 8 | tf_op jit(solution)/shard_map/psum | solution.py:217
  1389.0 72.6 %psum.62 = f32[]{:T(128)} all-reduce(f32[]{:T(128)} %multiply_reduce_fusion.38), channel_id=1, replica_groups=mesh['cam'=32,'pt'=8] {'cam','pt'}, use_global_device_ids=true, to_apply=%region_50.51 | all-reduce | flops 1 | bytes 8 | tf_op jit(solution)/shard_map/psum | solution.py:126
  1463.8 100.3 %all-gather.12.cloned.1.call-done = f32[9,32768]{1,0:T(8,128)} async-done(((f32[9,128]{1,0:T(8,128)}), f32[9,32768]{1,0:T(8,128)}) %all-gather.12.cloned.1.call-update) | async-done | bytes 1179664 | tf_op jit(solution)/shard_map/all_gather | solution.py:114
  1564.1 9.8 copy.778
  1573.9 8.4 gather_fusion.5
  1583.3 77.0 %psum.63 = f32[]{:T(128)} all-reduce(f32[]{:T(128)} %fusion.16), channel_id=1, replica_groups=mesh['cam'=32,'pt'=8] {'cam','pt'}, use_global_device_ids=true, to_apply=%region_52.53 | all-reduce | flops 1 | bytes 8 | tf_op jit(solution)/shard_map/psum | solution.py:217
  1663.0 99.2 %all-gather.14.cloned.1.call-done = f32[9,32768]{1,0:T(8,128)} async-done(((f32[9,128]{1,0:T(8,128)}), f32[9,32768]{1,0:T(8,128)}) %all-gather.14.cloned.1.call-update) | async-done | bytes 1179664 | tf_op jit(solution)/shard_map/all_gather | solution.py:224
  1762.2 9.8 copy.780
  1772.0 6.8 gather_fusion.9
  1779.0 6.8 gather_fusion.8
  1785.9 6.8 gather_fusion.7
  1792.7 6.8 gather_fusion.6
  (383 shorter events, 46.9 us)
Async XLA Ops:
  25.8 150.8 %copy-start.36 = (s32[4,4,512]{2,1,0:T(4,128)S(1)}, s32[4,4,512]{2,1,0:T(4,128)}, u32[]{:S(2)}) copy-start(s32[4,4,512]{2,1,0:T(4,128)} %param.17) | copy-start | bytes 98308
  25.8 195.1 %copy-start.34 = (s32[4,512]{1,0:T(4,128)S(1)}, s32[4,512]{1,0:T(4,128)}, u32[]{:S(2)}) copy-start(s32[4,512]{1,0:T(4,128)} %param.18) | copy-start | bytes 24580
  25.8 195.1 %copy-start.39 = (f32[4,2,512]{2,1,0:T(2,128)S(1)}, f32[4,2,512]{2,1,0:T(2,128)}, u32[]{:S(2)}) copy-start(f32[4,2,512]{2,1,0:T(2,128)} %param.14) | copy-start | bytes 49156
  25.8 195.1 %copy-start = (f32[4,18,512]{2,0,1:T(4,128)S(1)}, f32[4,18,512]{2,0,1:T(4,128)}, u32[]{:S(2)}) copy-start(f32[4,18,512]{2,0,1:T(4,128)} %param.12) | copy-start | bytes 442372
  25.8 195.5 %copy-start.24 = (f32[4,6,512]{2,0,1:T(4,128)S(1)}, f32[4,6,512]{2,0,1:T(4,128)}, u32[]{:S(2)}) copy-start(f32[4,6,512]{2,0,1:T(4,128)} %param.13) | copy-start | bytes 147460
  25.8 195.7 %copy-start.35 = (f32[9,512]{1,0:T(8,128)S(1)}, f32[9,512]{1,0:T(8,128)}, u32[]{:S(2)}) copy-start(f32[9,512]{1,0:T(8,128)} %param.15) | copy-start | bytes 55300
  176.6 44.8 %copy-start.37 = (s32[8192,1]{0,1:T(1,128)}, s32[8192,1]{0,1:T(1,128)S(1)}, u32[]{:S(2)}) copy-start(s32[8192,1]{0,1:T(1,128)S(1)} %compare_select_fusion.1) | copy-start | bytes 98308
  208.2 83.6 %all-to-all-start = ((s32[32,1,512]{2,1,0:T(1,128)}), s32[32,1,512]{2,1,0:T(1,128)}, u32[]{:S(2)}, u32[]{:S(2)}) async-start(s32[32,1,512]{2,1,0:T(1,128)} %reshape.8531), calls=%async_computation | async-start | bytes 131072 | tf_op jit(solution)/shard_map/all_to_all | solution.py:191
  221.6 4.1 copy-start.20
  223.3 7.4 copy-start.11
  223.3 7.4 copy-start.13
  223.3 7.4 copy-start.15
  223.4 7.4 copy-start.17
  250.5 3.8 copy-start.7
  250.5 3.8 copy-start.40
  250.5 3.9 copy-start.28
  250.5 3.9 copy-start.29
  250.5 3.9 copy-start.32
  250.5 3.9 copy-start.33
  252.0 6.6 copy-start.4
  253.5 8.9 copy-start.2
  253.6 9.8 copy-start.26
  254.3 7.2 copy-start.10
  254.3 9.1 copy-start.27
  254.3 9.1 copy-start.30
  254.3 9.1 copy-start.31
  254.3 9.2 copy-start.6
  254.4 9.3 copy-start.9
  254.4 9.3 copy-start.8
  254.5 9.3 copy-start.1
  254.5 9.3 copy-start.3
  255.7 8.1 copy-start.5
  291.8 200.5 %all-to-all-start.1 = ((f32[90,32,8,64]{0,3,2,1:T(8,128)}), f32[90,32,8,64]{0,3,2,1:T(8,128)}, u32[]{:S(2)}, u32[]{:S(2)}) async-start(f32[90,32,8,64]{0,3,2,1:T(8,128)} %bitcast.726), calls=%async_computation.1 | async-start | bytes 16777216 | tf_op jit(solution)/shard_map/all_to_all | solution.py:190
  301.1 331.6 %reduce-scatter.2.cloned.1.call-start = ((), (), s32[]{:S(2)}) async-start(), calls=%async_computation.3 | async-start | bytes 6635520 | tf_op jit(solution)/shard_map/reduce_scatter | solution.py:203
  591.1 45.9 %copy-start.41 = (s32[12,128]{1,0:T(8,128)S(1)}, s32[12,128]{1,0:T(8,128)}, u32[]{:S(2)}) copy-start(s32[12,128]{1,0:T(8,128)} %param.19) | copy-start | bytes 18436
  591.2 152.4 %all-gather.6.cloned.1.call-start = ((), (), s32[]{:S(2)}) async-start(), calls=%async_computation.4 | async-start | bytes 2105344 | tf_op jit(solution)/shard_map/all_gather | solution.py:114
  637.0 380.2 %all-gather.8.cloned.1.call-start = ((), (), s32[]{:S(2)}) async-start(), calls=%async_computation.5 | async-start | bytes 2105344 | tf_op jit(solution)/shard_map/all_gather | solution.py:114
  643.8 118.3 %copy-start.19 = (f32[9,128]{1,0:T(8,128)S(1)}, f32[9,128]{1,0:T(8,128)}, u32[]{:S(2)}) copy-start(f32[9,128]{1,0:T(8,128)} %stack.110) | copy-start | bytes 13828
  916.7 373.9 %all-gather.10.cloned.1.call-start = ((), (), s32[]{:S(2)}) async-start(), calls=%async_computation.6 | async-start | bytes 2105344 | tf_op jit(solution)/shard_map/all_gather | solution.py:114
  917.1 118.6 %copy-start.22 = (f32[9,128]{1,0:T(8,128)S(1)}, f32[9,128]{1,0:T(8,128)}, u32[]{:S(2)}) copy-start(f32[9,128]{1,0:T(8,128)} %multiply_add_fusion.7) | copy-start | bytes 13828
  1190.1 374.0 %all-gather.12.cloned.1.call-start = ((), (), s32[]{:S(2)}) async-start(), calls=%async_computation.7 | async-start | bytes 2105344 | tf_op jit(solution)/shard_map/all_gather | solution.py:114
  1190.3 118.9 %copy-start.23 = (f32[9,128]{1,0:T(8,128)S(1)}, f32[9,128]{1,0:T(8,128)}, u32[]{:S(2)}) copy-start(f32[9,128]{1,0:T(8,128)} %multiply_add_fusion.6) | copy-start | bytes 13828
  1463.6 298.6 %all-gather.14.cloned.1.call-start = ((), (), s32[]{:S(2)}) async-start(), calls=%async_computation.8 | async-start | bytes 2105344 | tf_op jit(solution)/shard_map/all_gather | solution.py:224
  1463.8 118.9 %copy-start.25 = (f32[9,128]{1,0:T(8,128)S(1)}, f32[9,128]{1,0:T(8,128)}, u32[]{:S(2)}) copy-start(f32[9,128]{1,0:T(8,128)} %multiply_add_fusion.5) | copy-start | bytes 13828
  1463.8 198.5 %copy-start.38 = (s32[4,512]{1,0:T(4,128)S(1)}, s32[4,512]{1,0:T(4,128)}, u32[]{:S(2)}) copy-start(s32[4,512]{1,0:T(4,128)} %param.16) | copy-start | bytes 24580
  1663.0 115.9 %copy-start.18 = (f32[1,9,3,512]{3,0,2,1:T(1,128)S(1)}, f32[1,9,3,512]{3,0,2,1:T(1,128)}, u32[]{:S(2)}) copy-start(f32[1,9,3,512]{3,0,2,1:T(1,128)} %copy-done.17) | copy-start | bytes 165892
  1663.0 122.9 %copy-start.16 = (f32[1,9,3,512]{3,0,2,1:T(1,128)S(1)}, f32[1,9,3,512]{3,0,2,1:T(1,128)}, u32[]{:S(2)}) copy-start(f32[1,9,3,512]{3,0,2,1:T(1,128)} %copy-done.15) | copy-start | bytes 165892
  1663.0 136.7 %copy-start.14 = (f32[1,9,3,512]{3,0,2,1:T(1,128)S(1)}, f32[1,9,3,512]{3,0,2,1:T(1,128)}, u32[]{:S(2)}) copy-start(f32[1,9,3,512]{3,0,2,1:T(1,128)} %copy-done.13) | copy-start | bytes 165892
  1663.0 136.8 %copy-start.12 = (f32[1,9,3,512]{3,0,2,1:T(1,128)S(1)}, f32[1,9,3,512]{3,0,2,1:T(1,128)}, u32[]{:S(2)}) copy-start(f32[1,9,3,512]{3,0,2,1:T(1,128)} %copy-done.11) | copy-start | bytes 165892
  1663.0 136.9 %copy-start.21 = (f32[3,3,512]{2,1,0:T(4,128)S(1)}, f32[3,3,512]{2,1,0:T(4,128)}, u32[]{:S(2)}) copy-start(f32[3,3,512]{2,1,0:T(4,128)} %copy-done.20) | copy-start | bytes 55300
Sparse Core Ops, SparseCore 0:
  591.3 41.3 reduce-scatter.1
  637.7 105.8 all-gather.5
  916.8 100.2 all-gather.7
  1190.2 100.3 all-gather.9
  1463.7 100.3 all-gather.11
  1662.4 99.7 all-gather.13
where the time goes:
time: 1810 us
  waiting for transfers between devices  730 us (40%)
  blocking collectives  526 us (29%)
  local copies, waits for them, and re-layouts  372 us (21%)
  other arithmetic  131 us (7%)
  between operations  25.4 us (1%)
  starting transfers between devices  22.4 us (1%)
    all_gather x4, waiting for transfers between devices, apply_schur(): whole = lax.all_gather(direction, ('cam', 'pt'), axis=1, tiled=True)  400 us
    psum x4, blocking collectives, energy_sum(): return lax.psum(jnp.sum(remainder * precond), ('cam', 'pt'))  295 us
    psum x3, blocking collectives, per_device(): alpha = energy_now / lax.psum(jnp.sum(direction * image), ('cam', 'pt'))  231 us
    all_to_all x1, waiting for transfers between devices, per_device(): lax.all_to_all(outgoing, 'cam', split_axis=1, concat_axis=1, tiled=True)  189 us
    gather x12, local copies, waits for them, and re-layouts, per_device(): starts = jnp.searchsorted(sorted_keys, sorted_keys, side='left')  141 us
    all_gather x1, waiting for transfers between devices, per_device(): whole_step = lax.all_gather(solution, ('cam', 'pt'), axis=1, tiled=True)  99.2 us
    scatter-add x1, other arithmetic, per_device(): buffer.at[:, cell_index.reshape(-1)]  90.8 us
    reduce_scatter x1, waiting for transfers between devices, per_device(): lax.psum_scatter(buffer.reshape(90, NBR + 1, n_pt * cam_dev), 'pt', scatt...  41.4 us
  transfers between devices with their start and end apart: 8, of which 7 were waited for; matrix products, arithmetic and copies ran while one was open for 4% of the time, Pallas kernels for 0%

commit v1 on v0

v1 whole, which is shorter than its diff:
```python
import functools

import jax
import jax.numpy as jnp
from jax import lax
from jax.experimental import pallas as pl
from jax.experimental.pallas import tpu as pltpu
from jax.sharding import PartitionSpec as P

TRACK = 4
NBR = 12
ITERS = 4
OBS_CAP = 16
DAMPING = 1.0
BOTH = ("cam", "pt")

GROUP = 14
PAIRS = 7
ROWS = 2
PAIR_ROWS = 3
CELL = 96
F32 = jnp.float32
BF16 = jnp.bfloat16
PARAMS = pltpu.CompilerParams(vmem_limit_bytes=48 * 1024 * 1024)


def iota(shape, dim):
    return lax.broadcasted_iota(jnp.int32, shape, dim)


def quotient(values, divisor):
    return jnp.floor((values.astype(F32) + 0.5) * (1.0 / divisor))


def pieces(values):
    high = values.astype(BF16)
    rest = values - high.astype(F32)
    middle = rest.astype(BF16)
    low = (rest - middle.astype(F32)).astype(BF16)
    return high, middle, low


def dot_nn(left, right):
    return lax.dot_general(left, right, (((1,), (0,)), ((), ())), preferred_element_type=F32)


def dot_nt(left, right):
    return lax.dot_general(left, right, (((1,), (1,)), ((), ())), preferred_element_type=F32)


def one_hot(condition):
    return jnp.where(condition, 1.0, 0.0).astype(BF16)


def before(size):
    return one_hot(iota((size, size), 0) < iota((size, size), 1))


def pack_kernel(
    devices, shift, jc_ref, jp_ref, rs_ref, vi_ref, cam_ref, slot_ref, used_ref, pattern_ref,
    out_ref, place_ref, rank_ref, feat_ref,
):
    npts = cam_ref.shape[1]
    cam_dev = pattern_ref.shape[1]
    found = jnp.zeros((devices, cam_dev), F32)
    for k in range(NBR):
        target = lax.shift_right_logical(pattern_ref[k : k + 1, :], shift)
        found = jnp.where(iota((devices, cam_dev), 0) == target, 1.0, found)
    rank = dot_nn(found.astype(BF16), before(cam_dev))
    rank_ref[...] = jnp.where(found > 0, rank, -1.0e6)

    live = [used_ref[a : a + 1, :].astype(F32) for a in range(TRACK)]
    carry = jnp.zeros((devices, 1), F32)
    triangle = before(npts)
    hits = []
    withins = []
    for a in range(TRACK):
        owner = lax.shift_right_logical(cam_ref[a : a + 1, :], shift)
        hit = jnp.where(
            jnp.logical_and(iota((devices, npts), 0) == owner, live[a] > 0), 1.0, 0.0
        )
        hits.append(hit.astype(BF16))
        count = dot_nn(hits[a], triangle) + carry
        within = jnp.sum(hit * count, axis=0, keepdims=True)
        carry = carry + jnp.sum(hit, axis=1, keepdims=True)
        withins.append(within)
        part = quotient(within, PAIRS)
        place_ref[a : a + 1, :] = jnp.where(live[a] > 0, owner.astype(F32) * PAIR_ROWS + part, -1.0)
        place_ref[TRACK + a : TRACK + a + 1, :] = within - part * PAIRS

    vi = [[vi_ref[3 * x + y : 3 * x + y + 1, :] for y in range(3)] for x in range(3)]
    jp = [
        [[jp_ref[a, 3 * u + x : 3 * u + x + 1, :] for x in range(3)] for u in range(2)]
        for a in range(TRACK)
    ]
    res = [[rs_ref[a, u : u + 1, :] for u in range(2)] for a in range(TRACK)]
    grad = []
    for x in range(3):
        total = jnp.zeros((1, npts), F32)
        for a in range(TRACK):
            total = total - live[a] * (jp[a][0][x] * res[a][0] + jp[a][1][x] * res[a][1])
        grad.append(total)
    for a in range(TRACK):
        at = slice(a * npts, (a + 1) * npts)
        for u in range(2):
            feat_ref[8 * u : 8 * u + 8, at] = jc_ref[a, 9 * u : 9 * u + 8, :]
            feat_ref[64 + u : 65 + u, at] = jc_ref[a, 9 * u + 8 : 9 * u + 9, :]
        removed = [
            [live[a] * sum(jp[a][u][x] * vi[x][y] for x in range(3)) for y in range(3)]
            for u in range(2)
        ]

        def middle(b, u, v):
            return -live[b] * sum(removed[u][y] * jp[b][v][y] for y in range(3))

        partners = [b for b in range(TRACK) if b != a]
        for m, b in enumerate(partners):
            first = [jc_ref[b, 9 * v : 9 * v + 8, :] for v in range(2)]
            ninth = [jc_ref[b, 9 * v + 8 : 9 * v + 9, :] for v in range(2)]
            for u in range(2):
                row = 2 + 2 * m + u
                one, two = middle(b, u, 0), middle(b, u, 1)
                feat_ref[8 * row : 8 * row + 8, at] = one * first[0] + two * first[1]
                feat_ref[64 + row : 65 + row, at] = one * ninth[0] + two * ninth[1]
        feat_ref[72:73, at] = live[a] + middle(a, 0, 0)
        feat_ref[73:74, at] = middle(a, 0, 1)
        feat_ref[74:75, at] = live[a] + middle(a, 1, 1)
        for u in range(2):
            right = -(live[a] * res[a][u] + sum(removed[u][y] * grad[y] for y in range(3)))
            feat_ref[75 + u : 76 + u, at] = right
        own = cam_ref[a : a + 1, :] & (cam_dev - 1)
        for m, b in enumerate(partners):
            label = slot_ref[a, b : b + 1, :] * cam_dev + own
            feat_ref[77 + m : 78 + m, at] = label.astype(F32)

    owners = jnp.concatenate(hits, axis=1)
    place = jnp.concatenate(withins, axis=1)
    split = pieces(feat_ref[...])
    masks = [
        one_hot(jnp.broadcast_to(place, (16, TRACK * npts)) == float(s)) for s in range(OBS_CAP)
    ]
    for g in range(5):
        for h in range(2):
            right = jnp.concatenate(
                [part[16 * g : 16 * g + 16] * masks[8 * h + c] for part in split for c in range(8)], axis=0
            )
            sums = dot_nt(owners, right)
            out_ref[pl.ds(2 * g + h, devices, stride=10), :] = (
                sums[:, :128] + sums[:, 128:256] + sums[:, 256:]
            )


def place_kernel(devices, shift, pattern_ref, source_ref, rank_ref):
    cam_dev = pattern_ref.shape[1]
    count = jnp.zeros((devices, cam_dev), F32)
    sources = []
    withins = []
    for k in range(NBR):
        camera = pattern_ref[k : k + 1, :]
        source = lax.shift_right_logical(camera, shift)
        within = camera & (cam_dev - 1)
        sources.append(iota((devices, cam_dev), 0) == source)
        withins.append(iota((cam_dev, cam_dev), 0) == within)
        count = count + dot_nt(one_hot(sources[k]), one_hot(withins[k]))
        source_ref[:, k * cam_dev : (k + 1) * cam_dev] = source.astype(F32)
    rank = dot_nn(one_hot(count > 0), before(cam_dev))
    turned = rank.T.astype(BF16)
    for k in range(NBR):
        column = dot_nn(turned, one_hot(sources[k]))
        rank_ref[:, k * cam_dev : (k + 1) * cam_dev] = jnp.sum(
            jnp.where(withins[k], column, 0.0), axis=0, keepdims=True
        )


def schur_kernel(got_ref, out_ref, wanted_ref, text_ref):
    devices = got_ref.shape[0] // 10
    cam_dev = out_ref.shape[2]
    chunk = 2 * devices
    out_ref[...] = jnp.zeros_like(out_ref)
    for h in range(2):
        for g in range(5):
            turned = got_ref[pl.ds(2 * g + h, devices, stride=10), :].T
            for c in range(8):
                text_ref[4 * h + c // 2, 16 * g : 16 * g + 16, (c % 2) * devices : (c % 2 + 1) * devices] = (
                    turned[16 * c : 16 * c + 16]
                )
    lines = []
    for s in range(OBS_CAP):
        label = text_ref[s // 2, 77:78, (s % 2) * devices : (s % 2 + 1) * devices]
        lines.append(label - cam_dev * quotient(label, cam_dev))
    lines.append(jnp.zeros((128 - OBS_CAP, devices), F32))
    wanted_ref[...] = jnp.concatenate(lines, axis=0).T

    def outer(left, right, extra):
        blocks = []
        for r in range(8):
            blocks.append(left[0][0][r : r + 1] * right[0][0] + left[1][0][r : r + 1] * right[1][0])
        blocks.append(left[0][1] * right[0][0] + left[1][1] * right[1][0])
        blocks.append(left[0][0] * right[0][1] + left[1][0] * right[1][1])
        corner = left[0][1] * right[0][1] + left[1][1] * right[1][1]
        if extra is None:
            blocks.append(jnp.concatenate([corner, jnp.zeros((7, chunk), F32)], axis=0))
            blocks.append(jnp.zeros((8, chunk), F32))
        else:
            last = left[0][1] * extra[0] + left[1][1] * extra[1]
            blocks.append(jnp.concatenate([corner, last, jnp.zeros((6, chunk), F32)], axis=0))
            blocks.append(left[0][0] * extra[0] + left[1][0] * extra[1])
        return jnp.concatenate(blocks, axis=0)

    def step(index, _):
        text = text_ref[index]
        vectors = [(text[8 * v : 8 * v + 8], text[64 + v : 65 + v]) for v in range(8)]
        own = vectors[0:2]
        cells = [quotient(text[77 + m : 78 + m], cam_dev) for m in range(3)]
        within = text[77:78] - cells[0] * cam_dev
        hit = one_hot(iota((cam_dev, chunk), 0).astype(F32) == within)
        corner = [[text[72:73], text[73:74]], [text[73:74], text[74:75]]]
        weighted = [
            tuple(corner[u][0] * own[0][i] + corner[u][1] * own[1][i] for i in range(2)) for u in range(2)
        ]
        terms = [outer(own, weighted, [text[75:76], text[76:77]])]
        for m in range(3):
            terms.append(outer(own, vectors[2 + 2 * m : 4 + 2 * m], None))
        terms = [jnp.concatenate(pieces(term), axis=0) for term in terms]
        for k in range(NBR + 1):
            if k < NBR:
                part = None
                for m in range(3):
                    piece = terms[1 + m] * one_hot(cells[m] == float(k))
                    part = piece if part is None else part + piece
            else:
                part = terms[0]
            sums = dot_nt(part, hit)
            out_ref[k] = out_ref[k] + (sums[:CELL] + sums[CELL : 2 * CELL] + sums[2 * CELL :])
        return 0

    lax.fori_loop(0, OBS_CAP // 2, step, 0)
    unit = iota((CELL, cam_dev), 0)
    unit = jnp.logical_and(unit <= 63, unit == 9 * lax.shift_right_logical(unit, 3)) | (unit == 80)
    out_ref[NBR] = out_ref[NBR] + jnp.where(unit, DAMPING, 0.0)


def cholesky(cells_ref, lower_ref):
    cam_dev = cells_ref.shape[2]
    zero = jnp.zeros((7, cam_dev), F32)
    block = cells_ref[NBR]
    columns = [
        jnp.concatenate([block[8 * r : 8 * r + 8], block[64 + r : 65 + r], zero], axis=0) for r in range(8)
    ]
    columns.append(jnp.concatenate([block[64:72], block[80:81], zero], axis=0))
    row = iota((16, cam_dev), 0)
    for c in range(9):
        pivot = columns[c][c : c + 1]
        root = jnp.sqrt(pivot)
        inverse = 1.0 / root
        column = jnp.where(row > c, columns[c] * inverse, 0.0)
        for r in range(c + 1, 9):
            columns[r] = columns[r] - column * column[r : r + 1]
        lower_ref[c] = jnp.where(row == 9, inverse, jnp.where(row < 9, column, 0.0))


def solve(lower_ref, vector):
    row = iota(vector.shape, 0)
    rest = vector
    copies = vector.shape[1] // lower_ref.shape[2]
    columns = [jnp.concatenate([lower_ref[c]] * copies, axis=1) for c in range(9)]
    for c in range(9):
        column = columns[c]
        value = rest[c : c + 1] * column[9:10]
        rest = jnp.where(row == c, value, rest - jnp.where(row < 9, column, 0.0) * value)
    for c in reversed(range(9)):
        column = columns[c]
        if c < 8:
            dotted = jnp.sum(
                jnp.where(jnp.logical_and(row > c, row < 9), column * rest, 0.0), axis=0, keepdims=True
            )
        else:
            dotted = jnp.zeros((1, vector.shape[1]), F32)
        value = (rest[c : c + 1] - dotted) * column[9:10]
        rest = jnp.where(row == c, value, rest)
    return rest


def multiply(cells_ref, taken, own):
    cam_dev = own.shape[1]
    sums = [jnp.zeros((8, cam_dev), F32) for _ in range(9)]
    side = jnp.zeros((8, cam_dev), F32)
    corner = jnp.zeros((1, cam_dev), F32)
    for k in range(NBR + 1):
        vector = own if k == NBR else taken[:, k * cam_dev : (k + 1) * cam_dev]
        first, last = vector[0:8], vector[8:9]
        for r in range(9):
            sums[r] = sums[r] + cells_ref[k, 8 * r : 8 * r + 8, :] * first
        side = side + cells_ref[k, 72:80, :] * last
        corner = corner + cells_ref[k, 80:81, :] * last
    lines = [jnp.sum(part, axis=0, keepdims=True) for part in sums]
    top = jnp.concatenate(lines[:8], axis=0) + side
    return jnp.concatenate([top, lines[8] + corner, jnp.zeros((7, cam_dev), F32)], axis=0)


def total_of(values):
    return jnp.sum(jnp.sum(values, axis=1, keepdims=True), axis=0, keepdims=True)


def spread(vector, row_of):
    cam_dev = vector.shape[1]
    choose = one_hot(iota((128, vector.shape[0]), 1).astype(F32) == row_of)
    copies = dot_nn(choose, jnp.concatenate(pieces(vector), axis=1))
    return [copies[:, p * cam_dev : (p + 1) * cam_dev] for p in range(3)]


def lane_groups(count):
    size = 126 // count
    lane = iota((128, 1), 0)
    group = quotient(lane, size)
    return group, lane.astype(F32) - group * size


def value_rows(count, values):
    if count == PAIRS:
        return jnp.where(values < 9, values, values + 7)
    return values


def send_rows(send_ref, vector, count, hits_of, rows, scalars):
    devices = send_ref.shape[0] // rows
    group, value = lane_groups(count)
    copies = spread(vector, value_rows(count, value))
    right = jnp.concatenate(
        [
            jnp.concatenate([jnp.where(group == float(g), part, 0.0) for g in range(count)], axis=1)
            for part in copies
        ],
        axis=0,
    ).astype(BF16)
    lane = iota((devices, 128), 1)
    for h in range(rows):
        hits = [hits_of(count * h + g) for g in range(count)]
        sums = dot_nt(jnp.concatenate(hits, axis=1), right)
        text = sums[:, :128] + sums[:, 128:256] + sums[:, 256:]
        for index, scalar in enumerate(scalars[2 * h : 2 * h + 2]):
            text = jnp.where(lane == 126 + index, scalar, text)
        send_ref[pl.ds(h, devices, stride=rows), :] = text


def send_coupled(send_ref, vector, count, rank_ref, rows, scalars):
    rank = rank_ref[...]
    send_rows(send_ref, vector, count, lambda slot: one_hot(rank == float(slot)), rows, scalars)


def read_rows(got, rows, count, places, groups, height, scalars):
    turned = got.T
    total = turned.shape[1]
    group, _ = lane_groups(count)
    mark = one_hot(iota((total, places.shape[1]), 0).astype(F32) == places)
    taken = dot_nn(jnp.concatenate(pieces(turned), axis=0), mark)
    wide = jnp.concatenate([group] * 3, axis=0)
    kept = jnp.where(wide == groups, taken, 0.0).astype(BF16)
    lane = iota((height, 128), 1)
    size = 126 // count
    value = value_rows(count, lane.astype(F32) - quotient(lane, size) * size)
    fold = one_hot(jnp.logical_and(iota((height, 128), 0).astype(F32) == value, lane < 126))
    vectors = dot_nn(jnp.concatenate([fold] * 3, axis=1), kept)
    column = iota((1, total), 1)
    inner = column.astype(F32) - quotient(column, rows) * rows
    sums = []
    for index in range(scalars):
        line = turned[126 + index % 2 : 127 + index % 2]
        sums.append(
            jnp.sum(jnp.where(inner == float(index // 2), line, 0.0), axis=1, keepdims=True)
        )
    return vectors, sums


def read_coupled(got_ref, rows, count, source_ref, rank_ref, height, scalars):
    part = quotient(rank_ref[...], count)
    places = source_ref[...] * rows + part
    return read_rows(got_ref[...], rows, count, places, rank_ref[...] - part * count, height, scalars)


def wide(index):
    return index >= 2


def layout(index):
    return (2 * ROWS, PAIRS) if wide(index) else (ROWS, GROUP)


def start_kernel(cells_ref, rank_ref, lower_ref, state_ref, send_ref):
    cam_dev = cells_ref.shape[2]
    cholesky(cells_ref, lower_ref)
    block = cells_ref[NBR]
    right = jnp.concatenate([block[88:96], block[81:82], jnp.zeros((7, cam_dev), F32)], axis=0)
    scaled = solve(lower_ref, right)
    zero = jnp.zeros_like(right)
    state_ref[0] = zero
    state_ref[1] = right
    state_ref[2] = scaled
    state_ref[3] = scaled
    state_ref[4] = zero
    state_ref[5] = zero
    state_ref[6] = zero
    most = jnp.max(jnp.max(rank_ref[...], axis=1, keepdims=True), axis=0, keepdims=True)
    crowded = jnp.where(most >= float(GROUP * ROWS), 1.0, 0.0)
    send_coupled(send_ref, scaled, GROUP, rank_ref, ROWS, [crowded])


def step_kernel(
    index, got_ref, source_ref, place_ref, rank_ref, cells_ref, lower_ref, state_ref, far_ref,
    state_out, far_out, send_ref,
):
    rows, count = layout(index)
    arrived, sums = read_coupled(
        got_ref, rows, count, source_ref, place_ref, 32 if wide(index) else 16, 4 if index else 1
    )
    cam_dev = cells_ref.shape[2]
    step, rest, scaled, direction = (state_ref[i] for i in range(4))
    if index:
        image, image_scaled = state_ref[4], state_ref[5]
        energy, cross, square, old = sums
        alpha = old / energy
        beta = (old - 2.0 * alpha * cross + alpha * alpha * square) / old
        step = step + alpha * direction
        rest = rest - alpha * image
        direction = (scaled - alpha * image_scaled) + beta * direction
        far_before = arrived[16:] if wide(index) else far_ref[...]
        far = (far_before - alpha * arrived[:16]) + beta * far_ref[...]
    else:
        far = arrived
    image = multiply(cells_ref, far, direction)
    energy = total_of(direction * image)
    state_out[0] = step
    state_out[1] = rest
    state_out[3] = direction
    state_out[4] = image
    state_out[6] = state_ref[6] if index else jnp.zeros_like(step) + sums[0]
    far_out[...] = far
    if index == ITERS - 1:
        scaled = solve(lower_ref, rest)
        state_out[2] = scaled
        state_out[5] = jnp.zeros_like(image)
        lane = iota((rank_ref.shape[0], cam_dev), 1).astype(F32)

        def wanted(slot):
            if slot < OBS_CAP:
                return one_hot(rank_ref[:, slot : slot + 1] == lane)
            return jnp.zeros(lane.shape, BF16)

        both = jnp.concatenate([step, direction], axis=0)
        send_rows(send_ref, both, PAIRS, wanted, PAIR_ROWS, [energy, total_of(rest * scaled)])
        return
    solved = solve(lower_ref, jnp.concatenate([rest, image], axis=1))
    scaled, image_scaled = solved[:, :cam_dev], solved[:, cam_dev:]
    state_out[2] = scaled
    state_out[5] = image_scaled
    scalars = [
        energy, total_of(scaled * image), total_of(image * image_scaled), total_of(rest * scaled)
    ]
    rows, count = layout(index + 1)
    vector = jnp.concatenate([image_scaled, scaled], axis=0) if wide(index + 1) else image_scaled
    send_coupled(send_ref, vector, count, rank_ref, rows, scalars)


def finish_kernel(
    got_ref, place_ref, state_ref, jc_ref, jp_ref, rs_ref, vi_ref, used_ref, step_ref, rest_ref, point_ref
):
    npts = used_ref.shape[1]
    places = jnp.concatenate([place_ref[a : a + 1, :] for a in range(TRACK)], axis=1)
    groups = jnp.concatenate([place_ref[TRACK + a : TRACK + a + 1, :] for a in range(TRACK)], axis=1)
    seen, sums = read_rows(got_ref[...], PAIR_ROWS, PAIRS, places, groups, 32, 2)
    alpha = sums[1] / sums[0]
    step_ref[...] = (state_ref[0] + alpha * state_ref[3])[:9]
    rest_ref[...] = (state_ref[1] - alpha * state_ref[4])[:9]
    moved = seen[:16] + alpha * seen[16:]
    reduced = [jnp.zeros((1, npts), F32) for _ in range(3)]
    for a in range(TRACK):
        live = used_ref[a : a + 1, :].astype(F32)
        there = moved[:9, a * npts : (a + 1) * npts]
        for u in range(2):
            change = jnp.sum(jc_ref[a, 9 * u : 9 * u + 9, :] * there, axis=0, keepdims=True)
            change = live * (change + rs_ref[a, u : u + 1, :])
            for x in range(3):
                reduced[x] = reduced[x] - jp_ref[a, 3 * u + x : 3 * u + x + 1, :] * change
    for x in range(3):
        point_ref[x : x + 1, :] = sum(
            vi_ref[3 * x + y : 3 * x + y + 1, :] * reduced[y] for y in range(3)
        )


def factor_blocks(matrix):
    lower = {}
    for row_idx in range(9):
        for col_idx in range(row_idx + 1):
            accum = matrix[row_idx, col_idx]
            for inner_idx in range(col_idx):
                accum = accum - lower[row_idx, inner_idx] * lower[col_idx, inner_idx]
            if row_idx == col_idx:
                lower[row_idx, row_idx] = jnp.sqrt(accum)
            else:
                lower[row_idx, col_idx] = accum / lower[col_idx, col_idx]
    return lower


def solve_blocks(lower, vector):
    forward = []
    for row_idx in range(9):
        accum = vector[row_idx]
        for inner_idx in range(row_idx):
            accum = accum - lower[row_idx, inner_idx] * forward[inner_idx]
        forward.append(accum / lower[row_idx, row_idx])
    backward = [None] * 9
    for row_idx in reversed(range(9)):
        accum = forward[row_idx]
        for inner_idx in range(row_idx + 1, 9):
            accum = accum - lower[inner_idx, row_idx] * backward[inner_idx]
        backward[row_idx] = accum / lower[row_idx, row_idx]
    return jnp.stack(backward)


def whole_exchange(cells, pattern, jacobian_cam, jacobian_pt, residuals, point_inverse, obs_camera, used):
    cam_dev = pattern.shape[1]
    main = cells[:, :64].reshape(NBR + 1, 8, 8, cam_dev)
    side = cells[:, 72:80].reshape(NBR + 1, 8, 1, cam_dev)
    foot = jnp.concatenate([cells[:, 64:72], cells[:, 80:81]], axis=1)[:, None]
    blocks = jnp.concatenate([jnp.concatenate([main, side], axis=2), foot], axis=1)
    gradient = jnp.concatenate([cells[NBR, 88:96], cells[NBR, 81:82]], axis=0)
    lower = factor_blocks(blocks[NBR])

    def gathered(vector):
        return lax.all_gather(vector, BOTH, axis=1, tiled=True)

    def summed(values):
        return lax.psum(jnp.sum(values), BOTH)

    step = jnp.zeros_like(gradient)
    rest = gradient
    scaled = solve_blocks(lower, rest)
    direction = scaled
    energy_now = summed(rest * scaled)
    for _ in range(ITERS):
        taken = jnp.concatenate([gathered(direction)[:, pattern], direction[:, None, :]], axis=1)
        image = jnp.sum(blocks * jnp.swapaxes(taken, 0, 1)[:, None], axis=(0, 2))
        alpha = energy_now / summed(direction * image)
        step = step + alpha * direction
        rest = rest - alpha * image
        scaled = solve_blocks(lower, rest)
        energy_next = summed(rest * scaled)
        direction = scaled + energy_next / energy_now * direction
        energy_now = energy_next
    whole = gathered(step)
    npts = obs_camera.shape[1]
    rows = jacobian_cam.reshape(TRACK, 2, 9, npts)
    seen = jnp.swapaxes(whole[:, obs_camera], 0, 1)
    change = jnp.sum(rows * seen[:, None], axis=2) + residuals
    change = change * used.astype(F32)[:, None]
    reduced = -jnp.sum(jacobian_pt.reshape(TRACK, 2, 3, npts) * change[:, :, None], axis=(0, 1))
    point_step = jnp.sum(point_inverse.reshape(3, 3, npts) * reduced[None], axis=1)
    return step, rest, point_step


def shape(*dims):
    return jax.ShapeDtypeStruct(dims, F32)


def call(kernel, outs, name, scratch=()):
    return pl.pallas_call(
        kernel, out_shape=outs, name=name, compiler_params=PARAMS, scratch_shapes=list(scratch)
    )


def exchange(message, devices):
    width = message.shape[0] // devices
    arrived = lax.all_to_all(
        message.reshape(devices, width, 1, 128), BOTH, split_axis=0, concat_axis=0, tiled=True
    )
    return arrived.reshape(devices * width, 128)


def per_device(
    jacobian_cam, jacobian_pt, residuals, point_inverse, obs_camera, pair_slot, observation_used, pattern,
):
    devices = lax.axis_size("cam") * lax.axis_size("pt")
    npts = obs_camera.shape[1]
    cam_dev = pattern.shape[1]
    shift = cam_dev.bit_length() - 1
    couplings = NBR * cam_dev

    packed, places, rank = call(
        functools.partial(pack_kernel, devices, shift),
        (shape(devices * 10, 128), shape(2 * TRACK, npts), shape(devices, cam_dev)),
        "pack",
        [pltpu.VMEM((80, TRACK * npts), F32)],
    )(jacobian_cam, jacobian_pt, residuals, point_inverse, obs_camera, pair_slot, observation_used, pattern)
    got = exchange(packed, devices)
    sources, far_rank = call(
        functools.partial(place_kernel, devices, shift),
        (shape(1, couplings), shape(1, couplings)),
        "place",
    )(pattern)
    cells, wanted = call(
        schur_kernel,
        (shape(NBR + 1, CELL, cam_dev), shape(devices, 128)),
        "schur",
        [pltpu.VMEM((OBS_CAP // 2, 80, 2 * devices), F32)],
    )(got)
    lower, state, message = call(
        start_kernel,
        (shape(9, 16, cam_dev), shape(7, 16, cam_dev), shape(devices * ROWS, 128)),
        "start",
    )(cells, rank)
    far = jnp.zeros((16, couplings), F32)
    crowded = None
    for index in range(ITERS):
        last = index == ITERS - 1
        rows = PAIR_ROWS if last else layout(index + 1)[0]
        arrived = exchange(message, devices)
        state, far, message = call(
            functools.partial(step_kernel, index),
            (shape(7, 16, cam_dev), shape(16, couplings), shape(devices * rows, 128)),
            "step",
        )(arrived, sources, far_rank, wanted if last else rank, cells, lower, state, far)
        if index == 0:
            crowded = state[6, 0, 0] > 0.0
    arrived = exchange(message, devices)
    found = call(
        finish_kernel, (shape(9, cam_dev), shape(9, cam_dev), shape(3, npts)), "finish"
    )(arrived, places, state, jacobian_cam, jacobian_pt, residuals, point_inverse, observation_used)

    def dense():
        return whole_exchange(
            cells, pattern, jacobian_cam, jacobian_pt, residuals, point_inverse, obs_camera, observation_used
        )

    return lax.cond(crowded, dense, lambda: tuple(found))


def solution(mesh):
    return jax.shard_map(
        per_device,
        mesh=mesh,
        in_specs=(
            P(None, None, BOTH),
            P(None, None, BOTH),
            P(None, None, BOTH),
            P(None, BOTH),
            P(None, BOTH),
            P(None, None, BOTH),
            P(None, BOTH),
            P(None, BOTH),
        ),
        out_specs=(P(None, BOTH), P(None, BOTH), P(None, BOTH)),
        check_vma=False,
    )
```

time: 1810 us -> 237 us (0.13)
  waiting for transfers between devices: 730 us -> 29.4 us
  blocking collectives: 526 us -> 137 us
  local copies, waits for them, and re-layouts: 372 us -> 4.25 us
  other arithmetic: 131 us -> 0 us
  Pallas kernels: 0 us -> 36.4 us
    psum x7 -> x0, blocking collectives: 526 us -> none  [the longest x4 295 us: energy_sum(): return lax.psum(jnp.sum(remainder * precond), ('cam', 'pt'))]
    all_gather x5 -> x0, waiting for transfers between devices: 500 us -> none  [the longest x4 400 us: apply_schur(): whole = lax.all_gather(direction, ('cam', 'pt'), axis=1, tiled=True)]
    gather x29 -> x0, local copies, waits for them, and re-layouts: 216 us -> none  [the longest x12 141 us: per_device(): starts = jnp.searchsorted(sorted_keys, sorted_keys, side='left')]
    all_to_all x2, waiting for transfers between devices: 189 us -> 29.4 us  [exchange(): lax.all_to_all(message.reshape(devices, width, 1, 128), BOTH, split_axis=...]
    all_to_all x0 -> x4, blocking collectives: none -> 137 us  [exchange(): lax.all_to_all(message.reshape(devices, width, 1, 128), BOTH, split_axis=...]
    scatter-add x1 -> x0, other arithmetic: 90.8 us -> none  [per_device(): buffer.at[:, cell_index.reshape(-1)]]
    scatter x3 -> x0, local copies, waits for them, and re-layouts: 63 us -> none  [the longest x1 30.5 us: per_device(): jnp.full((total_slots,), sentinel, jnp.int32).at[where_all]]
    all_gather x5 -> x0, local copies, waits for them, and re-layouts: 48.9 us -> none  [the longest x4 39.1 us: apply_schur(): whole = lax.all_gather(direction, ('cam', 'pt'), axis=1, tiled=True)]
  transfers between devices with their start and end apart: 8 -> 2, of which waited for: 7 -> 2; matrix products, arithmetic and copies ran while one was open for 4% -> 0% of each run, Pallas kernels for 0% -> 1%
where the time goes in v1:
time: 237 us; the launch traced here: 235 us
  blocking collectives  137 us (58%)
  Pallas kernels  36.4 us (15%)
  waiting for transfers between devices  29.4 us (12%)
  between operations  14.9 us (6%)
  starting transfers between devices  13 us (5%)
  local copies, waits for them, and re-layouts  4.25 us (2%)
    all_to_all x4, blocking collectives, exchange(): lax.all_to_all(message.reshape(devices, width, 1, 128), BOTH, split_axis=...  137 us
    all_to_all x2, waiting for transfers between devices, exchange(): lax.all_to_all(message.reshape(devices, width, 1, 128), BOTH, split_axis=...  29.4 us
    all_to_all x2, starting transfers between devices, exchange(): lax.all_to_all(message.reshape(devices, width, 1, 128), BOTH, split_axis=...  13 us
    pallas_call x4, Pallas kernels, per_device(): call(functools.partial(step_kernel, index), (shape(7, 16, cam_dev), shape...  11.5 us
    pallas_call x1, Pallas kernels, per_device(): call(schur_kernel, (shape(NBR + 1, CELL, cam_dev), shape(devices, 128)),...  10.9 us
    pallas_call x1, Pallas kernels, per_device(): call(functools.partial(pack_kernel, devices, shift), (shape(devices * 10,...  7.33 us
  transfers between devices with their start and end apart: 2, of which 2 were waited for; matrix products, arithmetic and copies ran while one was open for 0% of the time, Pallas kernels for 1%

profile of v1, /device:TPU:1, one launch (start us, length us, event | category | flops | bytes accessed | tf_op | source)
XLA Modules:
  0.0 235.0 jit_solution(3750311102228172579)
XLA Ops:
  7.2 1.0 copy.564.jc_ref
  8.1 0.8 copy.565.jp_ref
  8.9 0.0 copy-start
  9.0 0.7 copy-done
  9.7 7.3 %pack.1 = (f32[2560,128]{1,0:T(8,128)S(1)}, f32[8,512]{1,0:T(8,128)S(1)}, f32[256,128]{1,0:T(8,128)S(1)}) custom-call(f32[4,18,512]{2,1,0:T(8,128)S(1)} %copy.564.jc_ref, f32[4,6,512]{2,1,0:T(8,128)S(1)} %copy.565.jp_ref, f32[4,2,512]{2,1,0:T(2,128)} %rs_ref.3, f32[9,512]{1,0:T(8,128)} %vi_ref.3, s32[4,512]{1,0:T(4,128)} %cam_ref.1, ...), custom_call_target="tpu_custom_call" | custom-call | tf_op jit(solution)/shard_map/pack/pallas_call | solution.py:588
  17.0 51.5 %all_to_all.30 = f32[256,10,1,128]{3,2,1,0:T(1,128)S(1)} all-to-all(f32[256,10,1,128]{3,2,1,0:T(1,128)S(1)} %bitcast.596), channel_id=1, replica_groups=mesh['cam'=32,'pt'=8] {'cam','pt'}, dimensions={0} | all-to-all | bytes 2621440 | tf_op jit(solution)/shard_map/all_to_all | solution.py:573
  68.5 10.9 %schur.1 = (f32[13,96,128]{2,1,0:T(8,128)S(1)}, f32[256,128]{1,0:T(8,128)S(1)}) custom-call(f32[2560,128]{1,0:T(8,128)S(1)} %bitcast.592), custom_call_target="tpu_custom_call" | custom-call | tf_op jit(solution)/shard_map/schur/pallas_call | solution.py:600
  79.4 2.2 start.1
  81.7 6.9 %all-to-all-start.1 = ((f32[256,2,1,128]{3,1,2,0:T(2,128)}), f32[256,2,1,128]{3,1,2,0:T(2,128)S(1)}, u32[]{:S(2)}, u32[]{:S(2)}) async-start(f32[256,2,1,128]{3,1,2,0:T(2,128)} %bitcast.109), calls=%async_computation.1 | async-start | bytes 524288 | tf_op jit(solution)/shard_map/all_to_all | solution.py:573
  88.5 2.0 place.1
  90.5 13.4 %all-to-all-done.1 = f32[256,2,1,128]{3,1,2,0:T(2,128)S(1)} async-done(((f32[256,2,1,128]{3,1,2,0:T(2,128)}), f32[256,2,1,128]{3,1,2,0:T(2,128)S(1)}, u32[]{:S(2)}, u32[]{:S(2)}) %all-to-all-start.1) | async-done | bytes 262176 | tf_op jit(solution)/shard_map/all_to_all | solution.py:573
  103.9 2.4 %step.4 = (f32[7,16,128]{2,1,0:T(8,128)S(1)}, f32[16,1536]{1,0:T(8,128)S(1)}, f32[512,128]{1,0:T(8,128)S(1)}) custom-call(f32[512,128]{1,0:T(8,128)S(1)} %bitcast.597, f32[1,1536]{1,0:T(1,128)S(1)} %get-tuple-element.58.source_ref, f32[1,1536]{1,0:T(1,128)S(1)} %get-tuple-element.59.place_ref, f32[256,128]{1,0:T(8,128)S(1)} %get-tuple-element.56.rank_ref, ...), custom_call_target="tpu_custom_call" | custom-call | tf_op jit(solution)/shard_map/step/pallas_call | solution.py:617
  106.3 20.9 %all_to_all.31 = f32[256,2,1,128]{3,1,2,0:T(2,128)S(1)} all-to-all(f32[256,2,1,128]{3,1,2,0:T(2,128)S(1)} %bitcast.601), channel_id=1, replica_groups=mesh['cam'=32,'pt'=8] {'cam','pt'}, dimensions={0} | all-to-all | bytes 524288 | tf_op jit(solution)/shard_map/all_to_all | solution.py:573
  127.2 2.5 %step.5 = (f32[7,16,128]{2,1,0:T(8,128)S(1)}, f32[16,1536]{1,0:T(8,128)S(1)}, f32[1024,128]{1,0:T(8,128)S(1)}) custom-call(f32[512,128]{1,0:T(8,128)S(1)} %bitcast.598, f32[1,1536]{1,0:T(1,128)S(1)} %get-tuple-element.58.source_ref, f32[1,1536]{1,0:T(1,128)S(1)} %get-tuple-element.59.place_ref, f32[256,128]{1,0:T(8,128)S(1)} %get-tuple-element.56.rank_ref, ...), custom_call_target="tpu_custom_call" | custom-call | tf_op jit(solution)/shard_map/step/pallas_call | solution.py:617
  129.7 25.6 %all_to_all.32 = f32[256,4,1,128]{3,1,2,0:T(4,128)S(1)} all-to-all(f32[256,4,1,128]{3,1,2,0:T(4,128)S(1)} %bitcast.600), channel_id=1, replica_groups=mesh['cam'=32,'pt'=8] {'cam','pt'}, dimensions={0} | all-to-all | bytes 1048576 | tf_op jit(solution)/shard_map/all_to_all | solution.py:573
  155.3 3.2 %step.6 = (f32[7,16,128]{2,1,0:T(8,128)S(1)}, f32[16,1536]{1,0:T(8,128)S(1)}, f32[1024,128]{1,0:T(8,128)S(1)}) custom-call(f32[1024,128]{1,0:T(8,128)S(1)} %bitcast.594, f32[1,1536]{1,0:T(1,128)S(1)} %get-tuple-element.58.source_ref, f32[1,1536]{1,0:T(1,128)S(1)} %get-tuple-element.59.place_ref, f32[256,128]{1,0:T(8,128)S(1)} %get-tuple-element.56.rank_ref, ...), custom_call_target="tpu_custom_call" | custom-call | tf_op jit(solution)/shard_map/step/pallas_call | solution.py:617
  158.5 39.0 %all_to_all.33 = f32[256,4,1,128]{3,1,2,0:T(4,128)S(1)} all-to-all(f32[256,4,1,128]{3,1,2,0:T(4,128)S(1)} %bitcast.599), channel_id=1, replica_groups=mesh['cam'=32,'pt'=8] {'cam','pt'}, dimensions={0} | all-to-all | bytes 1048576 | tf_op jit(solution)/shard_map/all_to_all | solution.py:573
  197.5 3.4 %step.7 = (f32[7,16,128]{2,1,0:T(8,128)S(1)}, f32[16,1536]{1,0:T(8,128)}, f32[768,128]{1,0:T(8,128)}) custom-call(f32[1024,128]{1,0:T(8,128)S(1)} %bitcast.593, f32[1,1536]{1,0:T(1,128)S(1)} %get-tuple-element.58.source_ref, f32[1,1536]{1,0:T(1,128)S(1)} %get-tuple-element.59.place_ref, f32[256,128]{1,0:T(8,128)S(1)} %get-tuple-element.69.rank_ref, ...), custom_call_target="tpu_custom_call" | custom-call | tf_op jit(solution)/shard_map/step/pallas_call | solution.py:617
  200.9 6.2 %all-to-all-start.5 = ((f32[256,3,1,128]{3,2,1,0:T(1,128)}), f32[256,3,1,128]{3,2,1,0:T(1,128)S(1)}, u32[]{:S(2)}, u32[]{:S(2)}) async-start(f32[256,3,1,128]{3,2,1,0:T(1,128)} %bitcast.121), calls=%async_computation.5 | async-start | bytes 786432 | tf_op jit(solution)/shard_map/all_to_all | solution.py:573
  207.1 0.5 slice.280
  208.2 16.0 %all-to-all-done.5 = f32[256,3,1,128]{3,2,1,0:T(1,128)S(1)} async-done(((f32[256,3,1,128]{3,2,1,0:T(1,128)}), f32[256,3,1,128]{3,2,1,0:T(1,128)S(1)}, u32[]{:S(2)}, u32[]{:S(2)}) %all-to-all-start.5) | async-done | bytes 393248 | tf_op jit(solution)/shard_map/all_to_all | solution.py:573
  224.2 2.5 %finish.1 = (f32[9,128]{1,0:T(8,128)}, f32[9,128]{1,0:T(8,128)S(1)}, f32[3,512]{1,0:T(4,128)S(1)}) custom-call(f32[768,128]{1,0:T(8,128)S(1)} %bitcast.595, f32[8,512]{1,0:T(8,128)S(1)} %get-tuple-element.73.place_ref, f32[7,16,128]{2,1,0:T(8,128)S(1)} %get-tuple-element.74.state_ref, f32[4,18,512]{2,1,0:T(8,128)S(1)} %copy.564.jc_ref, ...), custom_call_target="tpu_custom_call" | custom-call | tf_op jit(solution)/shard_map/finish/pallas_call | solution.py:625
  226.7 0.0 copy-start.11
  226.7 0.6 copy-done.11
  227.3 0.0 copy-start.12
  227.3 0.6 copy-done.12
  (2 shorter events, 0.0 us)
Async XLA Ops:
  8.9 0.8 copy-start
  81.7 22.2 %all-to-all-start.1 = ((f32[256,2,1,128]{3,1,2,0:T(2,128)}), f32[256,2,1,128]{3,1,2,0:T(2,128)S(1)}, u32[]{:S(2)}, u32[]{:S(2)}) async-start(f32[256,2,1,128]{3,1,2,0:T(2,128)} %bitcast.109), calls=%async_computation.1 | async-start | bytes 524288 | tf_op jit(solution)/shard_map/all_to_all | solution.py:573
  200.9 23.4 %all-to-all-start.5 = ((f32[256,3,1,128]{3,2,1,0:T(1,128)}), f32[256,3,1,128]{3,2,1,0:T(1,128)S(1)}, u32[]{:S(2)}, u32[]{:S(2)}) async-start(f32[256,3,1,128]{3,2,1,0:T(1,128)} %bitcast.121), calls=%async_computation.5 | async-start | bytes 786432 | tf_op jit(solution)/shard_map/all_to_all | solution.py:573
  226.7 0.6 copy-start.11
  227.3 0.6 copy-start.12

commit v2 on v1

--- a/solution.py
+++ b/solution.py
@@ -21,7 +21,7 @@
 CELL = 96
 F32 = jnp.float32
 BF16 = jnp.bfloat16
-PARAMS = pltpu.CompilerParams(vmem_limit_bytes=48 * 1024 * 1024)
+PARAMS = pltpu.CompilerParams(vmem_limit_bytes=28 * 1024 * 1024)
 
 
 def iota(shape, dim):
@@ -90,7 +90,7 @@
 
     vi = [[vi_ref[3 * x + y : 3 * x + y + 1, :] for y in range(3)] for x in range(3)]
     jp = [
-        [[jp_ref[a, 3 * u + x : 3 * u + x + 1, :] for x in range(3)] for u in range(2)]
+        [[jp_ref[3 * u + x : 3 * u + x + 1, a, :] for x in range(3)] for u in range(2)]
         for a in range(TRACK)
     ]
     res = [[rs_ref[a, u : u + 1, :] for u in range(2)] for a in range(TRACK)]
@@ -103,8 +103,8 @@
     for a in range(TRACK):
         at = slice(a * npts, (a + 1) * npts)
         for u in range(2):
-            feat_ref[8 * u : 8 * u + 8, at] = jc_ref[a, 9 * u : 9 * u + 8, :]
-            feat_ref[64 + u : 65 + u, at] = jc_ref[a, 9 * u + 8 : 9 * u + 9, :]
+            feat_ref[8 * u : 8 * u + 8, at] = jc_ref[9 * u : 9 * u + 8, a, :]
+            feat_ref[64 + u : 65 + u, at] = jc_ref[9 * u + 8 : 9 * u + 9, a, :]
         removed = [
             [live[a] * sum(jp[a][u][x] * vi[x][y] for x in range(3)) for y in range(3)]
             for u in range(2)
@@ -115,8 +115,8 @@
 
         partners = [b for b in range(TRACK) if b != a]
         for m, b in enumerate(partners):
-            first = [jc_ref[b, 9 * v : 9 * v + 8, :] for v in range(2)]
-            ninth = [jc_ref[b, 9 * v + 8 : 9 * v + 9, :] for v in range(2)]
+            first = [jc_ref[9 * v : 9 * v + 8, b, :] for v in range(2)]
+            ninth = [jc_ref[9 * v + 8 : 9 * v + 9, b, :] for v in range(2)]
             for u in range(2):
                 row = 2 + 2 * m + u
                 one, two = middle(b, u, 0), middle(b, u, 1)
@@ -150,7 +150,7 @@
             )
 
 
-def place_kernel(devices, shift, pattern_ref, source_ref, rank_ref):
+def place_kernel(devices, shift, pattern_ref, source_ref, far_ref):
     cam_dev = pattern_ref.shape[1]
     count = jnp.zeros((devices, cam_dev), F32)
     sources = []
@@ -167,23 +167,100 @@
     turned = rank.T.astype(BF16)
     for k in range(NBR):
         column = dot_nn(turned, one_hot(sources[k]))
-        rank_ref[:, k * cam_dev : (k + 1) * cam_dev] = jnp.sum(
-            jnp.where(withins[k], column, 0.0), axis=0, keepdims=True
-        )
-
-
-def schur_kernel(got_ref, out_ref, wanted_ref, text_ref):
+        mine = jnp.sum(jnp.where(withins[k], column, 0.0), axis=0, keepdims=True)
+        far_ref[:, k * cam_dev : (k + 1) * cam_dev] = mine
+
+
+def outer(left, right, extra):
+    blocks = []
+    for r in range(8):
+        blocks.append(left[0][0][r : r + 1] * right[0][0] + left[1][0][r : r + 1] * right[1][0])
+    blocks.append(left[0][1] * right[0][0] + left[1][1] * right[1][0])
+    blocks.append(left[0][0] * right[0][1] + left[1][0] * right[1][1])
+    corner = left[0][1] * right[0][1] + left[1][1] * right[1][1]
+    chunk = corner.shape[1]
+    if extra is None:
+        blocks.append(jnp.concatenate([corner, jnp.zeros((7, chunk), F32)], axis=0))
+        blocks.append(jnp.zeros((8, chunk), F32))
+    else:
+        last = left[0][1] * extra[0] + left[1][1] * extra[1]
+        blocks.append(jnp.concatenate([corner, last, jnp.zeros((6, chunk), F32)], axis=0))
+        blocks.append(left[0][0] * extra[0] + left[1][0] * extra[1])
+    return jnp.concatenate(blocks, axis=0)
+
+
+def observation(text, cam_dev):
+    vectors = [(text[8 * v : 8 * v + 8], text[64 + v : 65 + v]) for v in range(8)]
+    cells = [quotient(text[77 + m : 78 + m], cam_dev) for m in range(3)]
+    within = text[77:78] - cells[0] * cam_dev
+    hit = one_hot(iota((cam_dev, text.shape[1]), 0).astype(F32) == within)
+    return vectors, cells, within, hit
+
+
+def folded(sums):
+    return sums[:CELL] + sums[CELL : 2 * CELL] + sums[2 * CELL :]
+
+
+def diagonal_kernel(
+    got_ref, rank_ref, text_ref, out_ref, lower_ref, state_ref, send_ref
+):
     devices = got_ref.shape[0] // 10
-    cam_dev = out_ref.shape[2]
-    chunk = 2 * devices
-    out_ref[...] = jnp.zeros_like(out_ref)
+    cam_dev = out_ref.shape[1]
     for h in range(2):
         for g in range(5):
             turned = got_ref[pl.ds(2 * g + h, devices, stride=10), :].T
             for c in range(8):
-                text_ref[4 * h + c // 2, 16 * g : 16 * g + 16, (c % 2) * devices : (c % 2 + 1) * devices] = (
-                    turned[16 * c : 16 * c + 16]
-                )
+                at = slice((c % 2) * devices, (c % 2 + 1) * devices)
+                text_ref[4 * h + c // 2, 16 * g : 16 * g + 16, at] = turned[16 * c : 16 * c + 16]
+    unit = iota((CELL, cam_dev), 0)
+    unit = jnp.logical_and(unit <= 63, unit == 9 * lax.shift_right_logical(unit, 3)) | (unit == 80)
+    total = jnp.where(unit, DAMPING, 0.0)
+    for index in range(OBS_CAP // 2):
+        text = text_ref[index]
+        vectors, _, _, hit = observation(text, cam_dev)
+        own = vectors[0:2]
+        corner = [[text[72:73], text[73:74]], [text[73:74], text[74:75]]]
+        weighted = [
+            tuple(corner[u][0] * own[0][i] + corner[u][1] * own[1][i] for i in range(2)) for u in range(2)
+        ]
+        term = outer(own, weighted, [text[75:76], text[76:77]])
+        total = total + folded(dot_nt(jnp.concatenate(pieces(term), axis=0), hit))
+    out_ref[...] = total
+    cholesky(out_ref, lower_ref)
+    right = jnp.concatenate([total[88:96], total[81:82], jnp.zeros((7, cam_dev), F32)], axis=0)
+    scaled = solve(lower_ref, right)
+    zero = jnp.zeros_like(right)
+    state_ref[0] = zero
+    state_ref[1] = right
+    state_ref[2] = scaled
+    state_ref[3] = scaled
+    for index in range(4, 7):
+        state_ref[index] = zero
+    most = jnp.max(jnp.max(rank_ref[...], axis=1, keepdims=True), axis=0, keepdims=True)
+    crowded = jnp.where(most >= float(GROUP * ROWS), 1.0, 0.0)
+    send_rows(send_ref, scaled, GROUP, ranked(rank_ref), ROWS, [crowded])
+
+
+def coupling_kernel(text_ref, out_ref, wanted_ref):
+    cam_dev = out_ref.shape[2]
+    devices = wanted_ref.shape[0]
+    out_ref[...] = jnp.zeros_like(out_ref)
+
+    def step(index, _):
+        vectors, cells, _, hit = observation(text_ref[index], cam_dev)
+        terms = [
+            jnp.concatenate(pieces(outer(vectors[0:2], vectors[2 + 2 * m : 4 + 2 * m], None)), axis=0)
+            for m in range(3)
+        ]
+        for k in range(NBR):
+            part = None
+            for m in range(3):
+                piece = terms[m] * one_hot(cells[m] == float(k))
+                part = piece if part is None else part + piece
+            out_ref[k] = out_ref[k] + folded(dot_nt(part, hit))
+        return 0
+
+    lax.fori_loop(0, OBS_CAP // 2, step, 0)
     lines = []
     for s in range(OBS_CAP):
         label = text_ref[s // 2, 77:78, (s % 2) * devices : (s % 2 + 1) * devices]
@@ -191,59 +268,11 @@
     lines.append(jnp.zeros((128 - OBS_CAP, devices), F32))
     wanted_ref[...] = jnp.concatenate(lines, axis=0).T
 
-    def outer(left, right, extra):
-        blocks = []
-        for r in range(8):
-            blocks.append(left[0][0][r : r + 1] * right[0][0] + left[1][0][r : r + 1] * right[1][0])
-        blocks.append(left[0][1] * right[0][0] + left[1][1] * right[1][0])
-        blocks.append(left[0][0] * right[0][1] + left[1][0] * right[1][1])
-        corner = left[0][1] * right[0][1] + left[1][1] * right[1][1]
-        if extra is None:
-            blocks.append(jnp.concatenate([corner, jnp.zeros((7, chunk), F32)], axis=0))
-            blocks.append(jnp.zeros((8, chunk), F32))
-        else:
-            last = left[0][1] * extra[0] + left[1][1] * extra[1]
-            blocks.append(jnp.concatenate([corner, last, jnp.zeros((6, chunk), F32)], axis=0))
-            blocks.append(left[0][0] * extra[0] + left[1][0] * extra[1])
-        return jnp.concatenate(blocks, axis=0)
-
-    def step(index, _):
-        text = text_ref[index]
-        vectors = [(text[8 * v : 8 * v + 8], text[64 + v : 65 + v]) for v in range(8)]
-        own = vectors[0:2]
-        cells = [quotient(text[77 + m : 78 + m], cam_dev) for m in range(3)]
-        within = text[77:78] - cells[0] * cam_dev
-        hit = one_hot(iota((cam_dev, chunk), 0).astype(F32) == within)
-        corner = [[text[72:73], text[73:74]], [text[73:74], text[74:75]]]
-        weighted = [
-            tuple(corner[u][0] * own[0][i] + corner[u][1] * own[1][i] for i in range(2)) for u in range(2)
-        ]
-        terms = [outer(own, weighted, [text[75:76], text[76:77]])]
-        for m in range(3):
-            terms.append(outer(own, vectors[2 + 2 * m : 4 + 2 * m], None))
-        terms = [jnp.concatenate(pieces(term), axis=0) for term in terms]
-        for k in range(NBR + 1):
-            if k < NBR:
-                part = None
-                for m in range(3):
-                    piece = terms[1 + m] * one_hot(cells[m] == float(k))
-                    part = piece if part is None else part + piece
-            else:
-                part = terms[0]
-            sums = dot_nt(part, hit)
-            out_ref[k] = out_ref[k] + (sums[:CELL] + sums[CELL : 2 * CELL] + sums[2 * CELL :])
-        return 0
-
-    lax.fori_loop(0, OBS_CAP // 2, step, 0)
-    unit = iota((CELL, cam_dev), 0)
-    unit = jnp.logical_and(unit <= 63, unit == 9 * lax.shift_right_logical(unit, 3)) | (unit == 80)
-    out_ref[NBR] = out_ref[NBR] + jnp.where(unit, DAMPING, 0.0)
-
 
 def cholesky(cells_ref, lower_ref):
-    cam_dev = cells_ref.shape[2]
+    cam_dev = cells_ref.shape[1]
     zero = jnp.zeros((7, cam_dev), F32)
-    block = cells_ref[NBR]
+    block = cells_ref[...]
     columns = [
         jnp.concatenate([block[8 * r : 8 * r + 8], block[64 + r : 65 + r], zero], axis=0) for r in range(8)
     ]
@@ -281,7 +310,7 @@
     return rest
 
 
-def multiply(cells_ref, taken, own):
+def multiply(cells_ref, diagonal_ref, taken, own):
     cam_dev = own.shape[1]
     sums = [jnp.zeros((8, cam_dev), F32) for _ in range(9)]
     side = jnp.zeros((8, cam_dev), F32)
@@ -289,10 +318,11 @@
     for k in range(NBR + 1):
         vector = own if k == NBR else taken[:, k * cam_dev : (k + 1) * cam_dev]
         first, last = vector[0:8], vector[8:9]
+        cell_ref = diagonal_ref if k == NBR else cells_ref.at[k]
         for r in range(9):
-            sums[r] = sums[r] + cells_ref[k, 8 * r : 8 * r + 8, :] * first
-        side = side + cells_ref[k, 72:80, :] * last
-        corner = corner + cells_ref[k, 80:81, :] * last
+            sums[r] = sums[r] + cell_ref[8 * r : 8 * r + 8, :] * first
+        side = side + cell_ref[72:80, :] * last
+        corner = corner + cell_ref[80:81, :] * last
     lines = [jnp.sum(part, axis=0, keepdims=True) for part in sums]
     top = jnp.concatenate(lines[:8], axis=0) + side
     return jnp.concatenate([top, lines[8] + corner, jnp.zeros((7, cam_dev), F32)], axis=0)
@@ -320,6 +350,11 @@
     if count == PAIRS:
         return jnp.where(values < 9, values, values + 7)
     return values
+
+
+def ranked(rank_ref):
+    rank = rank_ref[...]
+    return lambda slot: one_hot(rank == float(slot))
 
 
 def send_rows(send_ref, vector, count, hits_of, rows, scalars):
@@ -343,19 +378,14 @@
         send_ref[pl.ds(h, devices, stride=rows), :] = text
 
 
-def send_coupled(send_ref, vector, count, rank_ref, rows, scalars):
-    rank = rank_ref[...]
-    send_rows(send_ref, vector, count, lambda slot: one_hot(rank == float(slot)), rows, scalars)
-
-
 def read_rows(got, rows, count, places, groups, height, scalars):
     turned = got.T
     total = turned.shape[1]
     group, _ = lane_groups(count)
     mark = one_hot(iota((total, places.shape[1]), 0).astype(F32) == places)
     taken = dot_nn(jnp.concatenate(pieces(turned), axis=0), mark)
-    wide = jnp.concatenate([group] * 3, axis=0)
-    kept = jnp.where(wide == groups, taken, 0.0).astype(BF16)
+    group = jnp.concatenate([group] * 3, axis=0)
+    kept = jnp.where(group == groups, taken, 0.0).astype(BF16)
     lane = iota((height, 128), 1)
     size = 126 // count
     value = value_rows(count, lane.astype(F32) - quotient(lane, size) * size)
@@ -372,12 +402,6 @@
     return vectors, sums
 
 
-def read_coupled(got_ref, rows, count, source_ref, rank_ref, height, scalars):
-    part = quotient(rank_ref[...], count)
-    places = source_ref[...] * rows + part
-    return read_rows(got_ref[...], rows, count, places, rank_ref[...] - part * count, height, scalars)
-
-
 def wide(index):
     return index >= 2
 
@@ -386,32 +410,15 @@
     return (2 * ROWS, PAIRS) if wide(index) else (ROWS, GROUP)
 
 
-def start_kernel(cells_ref, rank_ref, lower_ref, state_ref, send_ref):
-    cam_dev = cells_ref.shape[2]
-    cholesky(cells_ref, lower_ref)
-    block = cells_ref[NBR]
-    right = jnp.concatenate([block[88:96], block[81:82], jnp.zeros((7, cam_dev), F32)], axis=0)
-    scaled = solve(lower_ref, right)
-    zero = jnp.zeros_like(right)
-    state_ref[0] = zero
-    state_ref[1] = right
-    state_ref[2] = scaled
-    state_ref[3] = scaled
-    state_ref[4] = zero
-    state_ref[5] = zero
-    state_ref[6] = zero
-    most = jnp.max(jnp.max(rank_ref[...], axis=1, keepdims=True), axis=0, keepdims=True)
-    crowded = jnp.where(most >= float(GROUP * ROWS), 1.0, 0.0)
-    send_coupled(send_ref, scaled, GROUP, rank_ref, ROWS, [crowded])
-
-
 def step_kernel(
-    index, got_ref, source_ref, place_ref, rank_ref, cells_ref, lower_ref, state_ref, far_ref,
+    index, got_ref, source_ref, place_ref, rank_ref, cells_ref, diagonal_ref, lower_ref, state_ref, far_ref,
     state_out, far_out, send_ref,
 ):
     rows, count = layout(index)
-    arrived, sums = read_coupled(
-        got_ref, rows, count, source_ref, place_ref, 32 if wide(index) else 16, 4 if index else 1
+    part = quotient(place_ref[...], count)
+    places, groups = source_ref[...] * rows + part, place_ref[...] - part * count
+    arrived, sums = read_rows(
+        got_ref[...], rows, count, places, groups, 32 if wide(index) else 16, 4 if index else 1
     )
     cam_dev = cells_ref.shape[2]
     step, rest, scaled, direction = (state_ref[i] for i in range(4))
@@ -427,7 +434,7 @@
         far = (far_before - alpha * arrived[:16]) + beta * far_ref[...]
     else:
         far = arrived
-    image = multiply(cells_ref, far, direction)
+    image = multiply(cells_ref, diagonal_ref, far, direction)
     energy = total_of(direction * image)
     state_out[0] = step
     state_out[1] = rest
@@ -458,7 +465,7 @@
     ]
     rows, count = layout(index + 1)
     vector = jnp.concatenate([image_scaled, scaled], axis=0) if wide(index + 1) else image_scaled
-    send_coupled(send_ref, vector, count, rank_ref, rows, scalars)
+    send_rows(send_ref, vector, count, ranked(rank_ref), rows, scalars)
 
 
 def finish_kernel(
@@ -477,10 +484,10 @@
         live = used_ref[a : a + 1, :].astype(F32)
         there = moved[:9, a * npts : (a + 1) * npts]
         for u in range(2):
-            change = jnp.sum(jc_ref[a, 9 * u : 9 * u + 9, :] * there, axis=0, keepdims=True)
+            change = jnp.sum(jc_ref[9 * u : 9 * u + 9, a, :] * there, axis=0, keepdims=True)
             change = live * (change + rs_ref[a, u : u + 1, :])
             for x in range(3):
-                reduced[x] = reduced[x] - jp_ref[a, 3 * u + x : 3 * u + x + 1, :] * change
+                reduced[x] = reduced[x] - jp_ref[3 * u + x : 3 * u + x + 1, a, :] * change
     for x in range(3):
         point_ref[x : x + 1, :] = sum(
             vi_ref[3 * x + y : 3 * x + y + 1, :] * reduced[y] for y in range(3)
@@ -517,8 +524,9 @@
     return jnp.stack(backward)
 
 
-def whole_exchange(cells, pattern, jacobian_cam, jacobian_pt, residuals, point_inverse, obs_camera, used):
+def whole_exchange(cells, diagonal, pattern, jacobian_cam, jacobian_pt, residuals, point_inverse, obs_camera, used):
     cam_dev = pattern.shape[1]
+    cells = jnp.concatenate([cells, diagonal[None]], axis=0)
     main = cells[:, :64].reshape(NBR + 1, 8, 8, cam_dev)
     side = cells[:, 72:80].reshape(NBR + 1, 8, 1, cam_dev)
     foot = jnp.concatenate([cells[:, 64:72], cells[:, 80:81]], axis=1)[:, None]
@@ -558,13 +566,15 @@
     return step, rest, point_step
 
 
-def shape(*dims):
-    return jax.ShapeDtypeStruct(dims, F32)
-
-
-def call(kernel, outs, name, scratch=()):
+def shape(*dims, dtype=F32):
+    return jax.ShapeDtypeStruct(dims, dtype)
+
+
+def call(kernel, outs, name, scratch=(), flops=0):
+    cost = pl.CostEstimate(flops=flops, bytes_accessed=1 << 20, transcendentals=0) if flops else None
     return pl.pallas_call(
-        kernel, out_shape=outs, name=name, compiler_params=PARAMS, scratch_shapes=list(scratch)
+        kernel, out_shape=outs, name=name, compiler_params=PARAMS, scratch_shapes=list(scratch),
+        cost_estimate=cost,
     )
 
 
@@ -585,29 +595,39 @@
     shift = cam_dev.bit_length() - 1
     couplings = NBR * cam_dev
 
+    cameras = jnp.transpose(jacobian_cam, (1, 0, 2))
+    points = jnp.transpose(jacobian_pt, (1, 0, 2))
+
     packed, places, rank = call(
         functools.partial(pack_kernel, devices, shift),
         (shape(devices * 10, 128), shape(2 * TRACK, npts), shape(devices, cam_dev)),
         "pack",
         [pltpu.VMEM((80, TRACK * npts), F32)],
-    )(jacobian_cam, jacobian_pt, residuals, point_inverse, obs_camera, pair_slot, observation_used, pattern)
+    )(cameras, points, residuals, point_inverse, obs_camera, pair_slot, observation_used, pattern)
     got = exchange(packed, devices)
     sources, far_rank = call(
         functools.partial(place_kernel, devices, shift),
         (shape(1, couplings), shape(1, couplings)),
         "place",
+        flops=4 * 10**9,
     )(pattern)
+    text, diagonal, lower, state, message = call(
+        diagonal_kernel,
+        (
+            shape(OBS_CAP // 2, 80, 2 * devices),
+            shape(CELL, cam_dev),
+            shape(9, 16, cam_dev),
+            shape(7, 16, cam_dev),
+            shape(devices * ROWS, 128),
+        ),
+        "diagonal",
+    )(got, rank)
     cells, wanted = call(
-        schur_kernel,
-        (shape(NBR + 1, CELL, cam_dev), shape(devices, 128)),
-        "schur",
-        [pltpu.VMEM((OBS_CAP // 2, 80, 2 * devices), F32)],
-    )(got)
-    lower, state, message = call(
-        start_kernel,
-        (shape(9, 16, cam_dev), shape(7, 16, cam_dev), shape(devices * ROWS, 128)),
-        "start",
-    )(cells, rank)
+        coupling_kernel,
+        (shape(NBR, CELL, cam_dev), shape(devices, 128)),
+        "coupling",
+        flops=8 * 10**9,
+    )(text)
     far = jnp.zeros((16, couplings), F32)
     crowded = None
     for index in range(ITERS):
@@ -618,17 +638,19 @@
             functools.partial(step_kernel, index),
             (shape(7, 16, cam_dev), shape(16, couplings), shape(devices * rows, 128)),
             "step",
-        )(arrived, sources, far_rank, wanted if last else rank, cells, lower, state, far)
+        )(
+            arrived, sources, far_rank, wanted if last else rank, cells, diagonal, lower, state, far
+        )
         if index == 0:
             crowded = state[6, 0, 0] > 0.0
     arrived = exchange(message, devices)
     found = call(
         finish_kernel, (shape(9, cam_dev), shape(9, cam_dev), shape(3, npts)), "finish"
-    )(arrived, places, state, jacobian_cam, jacobian_pt, residuals, point_inverse, observation_used)
+    )(arrived, places, state, cameras, points, residuals, point_inverse, observation_used)
 
     def dense():
         return whole_exchange(
-            cells, pattern, jacobian_cam, jacobian_pt, residuals, point_inverse, obs_camera, observation_used
+            cells, diagonal, pattern, jacobian_cam, jacobian_pt, residuals, point_inverse, obs_camera, observation_used
         )
 
     return lax.cond(crowded, dense, lambda: tuple(found))

time: 237 us -> 230 us (0.970)
  blocking collectives: 137 us -> 88.1 us
  waiting for transfers between devices: 29.4 us -> 55.4 us
  starting transfers between devices: 13 us -> 28.7 us
    all_to_all x4 -> x3, blocking collectives: 137 us -> 88.1 us  [exchange(): lax.all_to_all(message.reshape(devices, width, 1, 128), BOTH, split_axis=...]
    all_to_all x2 -> x3, waiting for transfers between devices: 29.4 us -> 55.4 us  [exchange(): lax.all_to_all(message.reshape(devices, width, 1, 128), BOTH, split_axis=...]
    all_to_all x2 -> x3, starting transfers between devices: 13 us -> 28.7 us  [exchange(): lax.all_to_all(message.reshape(devices, width, 1, 128), BOTH, split_axis=...]
  transfers between devices with their start and end apart: 2 -> 3, of which waited for: 2 -> 3; matrix products, arithmetic and copies ran while one was open for 0% -> 0% of each run, Pallas kernels for 1% -> 5%
where the time goes in v2:
time: 230 us; the launch traced here: 228 us
  blocking collectives  88.1 us (38%)
  waiting for transfers between devices  55.4 us (24%)
  Pallas kernels  38 us (17%)
  starting transfers between devices  28.7 us (12%)
  between operations  15 us (7%)
  local copies, waits for them, and re-layouts  2.51 us (1%)
    all_to_all x3, blocking collectives, exchange(): lax.all_to_all(message.reshape(devices, width, 1, 128), BOTH, split_axis=...  88.1 us
    all_to_all x3, waiting for transfers between devices, exchange(): lax.all_to_all(message.reshape(devices, width, 1, 128), BOTH, split_axis=...  55.4 us
    all_to_all x3, starting transfers between devices, exchange(): lax.all_to_all(message.reshape(devices, width, 1, 128), BOTH, split_axis=...  28.7 us
    pallas_call x4, Pallas kernels, per_device(): call(functools.partial(step_kernel, index), (shape(7, 16, cam_dev), shape...  11.5 us
    pallas_call x1, Pallas kernels, per_device(): call(coupling_kernel, (shape(NBR, CELL, cam_dev), shape(devices, 128)), '...  9.95 us
    pallas_call x1, Pallas kernels, per_device(): call(functools.partial(pack_kernel, devices, shift), (shape(devices * 10,...  8.62 us
  transfers between devices with their start and end apart: 3, of which 3 were waited for; matrix products, arithmetic and copies ran while one was open for 0% of the time, Pallas kernels for 5%

profile of v2, /device:TPU:1, one launch (start us, length us, event | category | flops | bytes accessed | tf_op | source)
XLA Modules:
  0.0 227.7 jit_solution(5244525112062813443)
XLA Ops:
  7.2 0.0 copy-start
  7.2 0.7 copy-done
  7.9 8.6 %pack.1 = (f32[2560,128]{1,0:T(8,128)}, f32[8,512]{1,0:T(8,128)S(1)}, f32[256,128]{1,0:T(8,128)S(1)}) custom-call(f32[18,4,512]{2,1,0:T(4,128)} %bitcast.620, f32[6,4,512]{2,1,0:T(4,128)} %bitcast.628, f32[4,2,512]{2,1,0:T(2,128)} %rs_ref.3, f32[9,512]{1,0:T(8,128)} %vi_ref.3, s32[4,512]{1,0:T(4,128)} %cam_ref.1, s32[4,4,512]{2,1,0:T(4,128)S(1)} %copy-done, ...), custom_call_target="tpu_custom_call" | custom-call | tf_op jit(solution)/shard_map/pack/pallas_call | solution.py:601
  16.5 15.7 %all-to-all-start = ((f32[256,10,1,128]{3,2,1,0:T(1,128)}), f32[256,10,1,128]{3,2,1,0:T(1,128)S(1)}, u32[]{:S(2)}, u32[]{:S(2)}) async-start(f32[256,10,1,128]{3,2,1,0:T(1,128)} %bitcast.111), calls=%async_computation | async-start | bytes 2621440 | tf_op jit(solution)/shard_map/all_to_all | solution.py:583
  32.2 2.0 place.1
  34.2 34.0 %all-to-all-done = f32[256,10,1,128]{3,2,1,0:T(1,128)S(1)} async-done(((f32[256,10,1,128]{3,2,1,0:T(1,128)}), f32[256,10,1,128]{3,2,1,0:T(1,128)S(1)}, u32[]{:S(2)}, u32[]{:S(2)}) %all-to-all-start) | async-done | bytes 1310752 | tf_op jit(solution)/shard_map/all_to_all | solution.py:583
  68.2 4.3 %diagonal.1 = (f32[8,80,512]{2,1,0:T(8,128)S(1)}, f32[96,128]{1,0:T(8,128)S(1)}, f32[9,16,128]{2,1,0:T(8,128)S(1)}, f32[7,16,128]{2,1,0:T(8,128)S(1)}, f32[512,128]{1,0:T(8,128)}) custom-call(f32[2560,128]{1,0:T(8,128)S(1)} %bitcast.597, f32[256,128]{1,0:T(8,128)S(1)} %get-tuple-element.60.rank_ref), custom_call_target="tpu_custom_call" | custom-call | tf_op jit(solution)/shard_map/diagonal/pallas_call | solution.py:614
  72.5 6.9 %all-to-all-start.1 = ((f32[256,2,1,128]{3,1,2,0:T(2,128)}), f32[256,2,1,128]{3,1,2,0:T(2,128)S(1)}, u32[]{:S(2)}, u32[]{:S(2)}) async-start(f32[256,2,1,128]{3,1,2,0:T(2,128)} %bitcast.114), calls=%async_computation.1 | async-start | bytes 524288 | tf_op jit(solution)/shard_map/all_to_all | solution.py:583
  79.3 0.0 copy-start.1
  79.4 0.0 copy-start.2
  79.4 0.0 copy-start.3
  79.4 0.0 copy-start.7
  79.4 0.0 copy-start.9
  79.4 0.0 copy-start.10
  79.4 0.0 copy-start.11
  79.4 10.0 %coupling.1 = (f32[12,96,128]{2,1,0:T(8,128)S(1)}, f32[256,128]{1,0:T(8,128)S(1)}) custom-call(f32[8,80,512]{2,1,0:T(8,128)S(1)} %get-tuple-element.64.text_ref), custom_call_target="tpu_custom_call" | custom-call | flops 8000000000 | bytes 1048576 | tf_op jit(solution)/shard_map/coupling/pallas_call | solution.py:625
  89.4 5.3 %all-to-all-done.1 = f32[256,2,1,128]{3,1,2,0:T(2,128)S(1)} async-done(((f32[256,2,1,128]{3,1,2,0:T(2,128)}), f32[256,2,1,128]{3,1,2,0:T(2,128)S(1)}, u32[]{:S(2)}, u32[]{:S(2)}) %all-to-all-start.1) | async-done | bytes 262176 | tf_op jit(solution)/shard_map/all_to_all | solution.py:583
  94.7 2.4 %step.4 = (f32[7,16,128]{2,1,0:T(8,128)S(1)}, f32[16,1536]{1,0:T(8,128)S(1)}, f32[512,128]{1,0:T(8,128)S(1)}) custom-call(f32[512,128]{1,0:T(8,128)S(1)} %bitcast.601, f32[1,1536]{1,0:T(1,128)S(1)} %get-tuple-element.62.source_ref, f32[1,1536]{1,0:T(1,128)S(1)} %get-tuple-element.63.place_ref, f32[256,128]{1,0:T(8,128)S(1)} %get-tuple-element.60.rank_ref, ...), custom_call_target="tpu_custom_call" | custom-call | tf_op jit(solution)/shard_map/step/pallas_call | solution.py:637
  97.2 23.6 %all_to_all.30 = f32[256,2,1,128]{3,1,2,0:T(2,128)S(1)} all-to-all(f32[256,2,1,128]{3,1,2,0:T(2,128)S(1)} %bitcast.605), channel_id=1, replica_groups=mesh['cam'=32,'pt'=8] {'cam','pt'}, dimensions={0} | all-to-all | bytes 524288 | tf_op jit(solution)/shard_map/all_to_all | solution.py:583
  120.7 2.5 %step.5 = (f32[7,16,128]{2,1,0:T(8,128)S(1)}, f32[16,1536]{1,0:T(8,128)S(1)}, f32[1024,128]{1,0:T(8,128)S(1)}) custom-call(f32[512,128]{1,0:T(8,128)S(1)} %bitcast.602, f32[1,1536]{1,0:T(1,128)S(1)} %get-tuple-element.62.source_ref, f32[1,1536]{1,0:T(1,128)S(1)} %get-tuple-element.63.place_ref, f32[256,128]{1,0:T(8,128)S(1)} %get-tuple-element.60.rank_ref, ...), custom_call_target="tpu_custom_call" | custom-call | tf_op jit(solution)/shard_map/step/pallas_call | solution.py:637
  123.3 25.6 %all_to_all.31 = f32[256,4,1,128]{3,1,2,0:T(4,128)S(1)} all-to-all(f32[256,4,1,128]{3,1,2,0:T(4,128)S(1)} %bitcast.604), channel_id=1, replica_groups=mesh['cam'=32,'pt'=8] {'cam','pt'}, dimensions={0} | all-to-all | bytes 1048576 | tf_op jit(solution)/shard_map/all_to_all | solution.py:583
  148.9 3.2 %step.6 = (f32[7,16,128]{2,1,0:T(8,128)S(1)}, f32[16,1536]{1,0:T(8,128)S(1)}, f32[1024,128]{1,0:T(8,128)S(1)}) custom-call(f32[1024,128]{1,0:T(8,128)S(1)} %bitcast.599, f32[1,1536]{1,0:T(1,128)S(1)} %get-tuple-element.62.source_ref, f32[1,1536]{1,0:T(1,128)S(1)} %get-tuple-element.63.place_ref, f32[256,128]{1,0:T(8,128)S(1)} %get-tuple-element.60.rank_ref, ...), custom_call_target="tpu_custom_call" | custom-call | tf_op jit(solution)/shard_map/step/pallas_call | solution.py:637
  152.0 39.0 %all_to_all.32 = f32[256,4,1,128]{3,1,2,0:T(4,128)S(1)} all-to-all(f32[256,4,1,128]{3,1,2,0:T(4,128)S(1)} %bitcast.603), channel_id=1, replica_groups=mesh['cam'=32,'pt'=8] {'cam','pt'}, dimensions={0} | all-to-all | bytes 1048576 | tf_op jit(solution)/shard_map/all_to_all | solution.py:583
  191.0 3.4 %step.7 = (f32[7,16,128]{2,1,0:T(8,128)S(1)}, f32[16,1536]{1,0:T(8,128)}, f32[768,128]{1,0:T(8,128)}) custom-call(f32[1024,128]{1,0:T(8,128)S(1)} %bitcast.598, f32[1,1536]{1,0:T(1,128)S(1)} %get-tuple-element.62.source_ref, f32[1,1536]{1,0:T(1,128)S(1)} %get-tuple-element.63.place_ref, f32[256,128]{1,0:T(8,128)S(1)} %get-tuple-element.76.rank_ref, ...), custom_call_target="tpu_custom_call" | custom-call | tf_op jit(solution)/shard_map/step/pallas_call | solution.py:637
  194.4 6.2 %all-to-all-start.5 = ((f32[256,3,1,128]{3,2,1,0:T(1,128)}), f32[256,3,1,128]{3,2,1,0:T(1,128)S(1)}, u32[]{:S(2)}, u32[]{:S(2)}) async-start(f32[256,3,1,128]{3,2,1,0:T(1,128)} %bitcast.126), calls=%async_computation.5 | async-start | bytes 786432 | tf_op jit(solution)/shard_map/all_to_all | solution.py:583
  200.6 0.5 slice.280
  201.7 16.0 %all-to-all-done.5 = f32[256,3,1,128]{3,2,1,0:T(1,128)S(1)} async-done(((f32[256,3,1,128]{3,2,1,0:T(1,128)}), f32[256,3,1,128]{3,2,1,0:T(1,128)S(1)}, u32[]{:S(2)}, u32[]{:S(2)}) %all-to-all-start.5) | async-done | bytes 393248 | tf_op jit(solution)/shard_map/all_to_all | solution.py:583
  217.7 0.0 copy-done.1
  217.7 0.0 copy-done.2
  217.7 0.0 copy-done.3
  217.7 0.0 copy-done.7
  217.7 0.0 copy-done.9
  217.7 1.7 finish.1
  219.5 0.0 copy-done.10
  219.5 0.0 copy-done.11
  219.5 0.0 copy-start.12
  219.5 0.6 copy-done.12
  220.1 0.0 copy-start.13
  220.1 0.6 copy-done.13
  (2 shorter events, 0.0 us)
Async XLA Ops:
  7.2 0.8 copy-start
  16.5 51.7 %all-to-all-start = ((f32[256,10,1,128]{3,2,1,0:T(1,128)}), f32[256,10,1,128]{3,2,1,0:T(1,128)S(1)}, u32[]{:S(2)}, u32[]{:S(2)}) async-start(f32[256,10,1,128]{3,2,1,0:T(1,128)} %bitcast.111), calls=%async_computation | async-start | bytes 2621440 | tf_op jit(solution)/shard_map/all_to_all | solution.py:583
  72.5 22.2 %all-to-all-start.1 = ((f32[256,2,1,128]{3,1,2,0:T(2,128)}), f32[256,2,1,128]{3,1,2,0:T(2,128)S(1)}, u32[]{:S(2)}, u32[]{:S(2)}) async-start(f32[256,2,1,128]{3,1,2,0:T(2,128)} %bitcast.114), calls=%async_computation.1 | async-start | bytes 524288 | tf_op jit(solution)/shard_map/all_to_all | solution.py:583
  79.3 138.4 %copy-start.1 = (f32[4,18,512]{2,0,1:T(4,128)S(1)}, f32[4,18,512]{2,0,1:T(4,128)}, u32[]{:S(2)}) copy-start(f32[4,18,512]{2,0,1:T(4,128)} %param.10) | copy-start | bytes 442372
  79.4 138.4 %copy-start.2 = (f32[4,6,512]{2,0,1:T(4,128)S(1)}, f32[4,6,512]{2,0,1:T(4,128)}, u32[]{:S(2)}) copy-start(f32[4,6,512]{2,0,1:T(4,128)} %param.11) | copy-start | bytes 147460
  79.4 138.4 %copy-start.3 = (f32[9,512]{1,0:T(8,128)S(1)}, f32[9,512]{1,0:T(8,128)}, u32[]{:S(2)}) copy-start(f32[9,512]{1,0:T(8,128)} %vi_ref.3) | copy-start | bytes 55300
  79.4 138.3 %copy-start.7 = (f32[4,2,512]{2,1,0:T(2,128)S(1)}, f32[4,2,512]{2,1,0:T(2,128)}, u32[]{:S(2)}) copy-start(f32[4,2,512]{2,1,0:T(2,128)} %rs_ref.3) | copy-start | bytes 49156
  79.4 138.3 %copy-start.9 = (s32[4,512]{1,0:T(4,128)S(1)}, s32[4,512]{1,0:T(4,128)}, u32[]{:S(2)}) copy-start(s32[4,512]{1,0:T(4,128)} %used_ref.3) | copy-start | bytes 24580
  79.4 140.1 %copy-start.10 = (s32[4,512]{1,0:T(4,128)S(1)}, s32[4,512]{1,0:T(4,128)}, u32[]{:S(2)}) copy-start(s32[4,512]{1,0:T(4,128)} %cam_ref.1) | copy-start | bytes 24580
  79.4 140.1 %copy-start.11 = (s32[12,128]{1,0:T(8,128)S(1)}, s32[12,128]{1,0:T(8,128)}, u32[]{:S(2)}) copy-start(s32[12,128]{1,0:T(8,128)} %pattern_ref.3) | copy-start | bytes 18436
  194.4 23.3 %all-to-all-start.5 = ((f32[256,3,1,128]{3,2,1,0:T(1,128)}), f32[256,3,1,128]{3,2,1,0:T(1,128)S(1)}, u32[]{:S(2)}, u32[]{:S(2)}) async-start(f32[256,3,1,128]{3,2,1,0:T(1,128)} %bitcast.126), calls=%async_computation.5 | async-start | bytes 786432 | tf_op jit(solution)/shard_map/all_to_all | solution.py:583
  219.5 0.6 copy-start.12
  220.1 0.6 copy-start.13

commit v3 on v2

--- a/solution.py
+++ b/solution.py
@@ -17,6 +17,8 @@
 GROUP = 14
 PAIRS = 7
 ROWS = 2
+SLOTS = GROUP * ROWS
+CARRIED = 32
 PAIR_ROWS = 3
 CELL = 96
 F32 = jnp.float32
@@ -56,9 +58,23 @@
     return one_hot(iota((size, size), 0) < iota((size, size), 1))
 
 
+def flat(array):
+    tracks, rows, npts = array.shape
+    tiles = jnp.transpose(array, (1, 0, 2)).reshape(rows, tracks, npts // 128, 128)
+    return jnp.transpose(tiles, (0, 2, 1, 3)).reshape(-1, 128)
+
+
+def lines(ref, a, first, count, npts):
+    tiles = npts // 128
+    step = TRACK * tiles
+    return jnp.concatenate(
+        [ref[pl.ds(step * first + TRACK * t + a, count, stride=step), :] for t in range(tiles)], axis=1
+    )
+
+
 def pack_kernel(
     devices, shift, jc_ref, jp_ref, rs_ref, vi_ref, cam_ref, slot_ref, used_ref, pattern_ref,
-    out_ref, place_ref, rank_ref, feat_ref,
+    out_ref, place_ref, rank_ref, back_ref, feat_ref,
 ):
     npts = cam_ref.shape[1]
     cam_dev = pattern_ref.shape[1]
@@ -68,6 +84,9 @@
         found = jnp.where(iota((devices, cam_dev), 0) == target, 1.0, found)
     rank = dot_nn(found.astype(BF16), before(cam_dev))
     rank_ref[...] = jnp.where(found > 0, rank, -1.0e6)
+    back = SLOTS - 1.0 - rank
+    most = jnp.sum(found, axis=1, keepdims=True)
+    back_ref[...] = jnp.where(jnp.logical_and(found > 0, back >= most), back, -1.0e6)
 
     live = [used_ref[a : a + 1, :].astype(F32) for a in range(TRACK)]
     carry = jnp.zeros((devices, 1), F32)
@@ -90,9 +109,10 @@
 
     vi = [[vi_ref[3 * x + y : 3 * x + y + 1, :] for y in range(3)] for x in range(3)]
     jp = [
-        [[jp_ref[3 * u + x : 3 * u + x + 1, a, :] for x in range(3)] for u in range(2)]
-        for a in range(TRACK)
+        [[gradient[3 * u + x : 3 * u + x + 1] for x in range(3)] for u in range(2)]
+        for gradient in [lines(jp_ref, a, 0, 6, npts) for a in range(TRACK)]
     ]
+    jc = [lines(jc_ref, a, 0, 18, npts) for a in range(TRACK)]
     res = [[rs_ref[a, u : u + 1, :] for u in range(2)] for a in range(TRACK)]
     grad = []
     for x in range(3):
@@ -103,8 +123,8 @@
     for a in range(TRACK):
         at = slice(a * npts, (a + 1) * npts)
         for u in range(2):
-            feat_ref[8 * u : 8 * u + 8, at] = jc_ref[9 * u : 9 * u + 8, a, :]
-            feat_ref[64 + u : 65 + u, at] = jc_ref[9 * u + 8 : 9 * u + 9, a, :]
+            feat_ref[8 * u : 8 * u + 8, at] = jc[a][9 * u : 9 * u + 8]
+            feat_ref[64 + u : 65 + u, at] = jc[a][9 * u + 8 : 9 * u + 9]
         removed = [
             [live[a] * sum(jp[a][u][x] * vi[x][y] for x in range(3)) for y in range(3)]
             for u in range(2)
@@ -115,8 +135,8 @@
 
         partners = [b for b in range(TRACK) if b != a]
         for m, b in enumerate(partners):
-            first = [jc_ref[9 * v : 9 * v + 8, b, :] for v in range(2)]
-            ninth = [jc_ref[9 * v + 8 : 9 * v + 9, b, :] for v in range(2)]
+            first = [jc[b][9 * v : 9 * v + 8] for v in range(2)]
+            ninth = [jc[b][9 * v + 8 : 9 * v + 9] for v in range(2)]
             for u in range(2):
                 row = 2 + 2 * m + u
                 one, two = middle(b, u, 0), middle(b, u, 1)
@@ -140,17 +160,22 @@
         one_hot(jnp.broadcast_to(place, (16, TRACK * npts)) == float(s)) for s in range(OBS_CAP)
     ]
     for g in range(5):
+        right = jnp.concatenate(
+            [
+                part[16 * g : 16 * g + 16] * masks[8 * h + c]
+                for h in range(2) for part in split for c in range(8)
+            ],
+            axis=0,
+        )
+        sums = dot_nt(owners, right)
         for h in range(2):
-            right = jnp.concatenate(
-                [part[16 * g : 16 * g + 16] * masks[8 * h + c] for part in split for c in range(8)], axis=0
+            mine = sums[:, 384 * h : 384 * h + 384]
+            out_ref[pl.ds(2 * g + h, devices, stride=10), :] = (
+                mine[:, :128] + mine[:, 128:256] + mine[:, 256:]
             )
-            sums = dot_nt(owners, right)
-            out_ref[pl.ds(2 * g + h, devices, stride=10), :] = (
-                sums[:, :128] + sums[:, 128:256] + sums[:, 256:]
-            )
-
-
-def place_kernel(devices, shift, pattern_ref, source_ref, far_ref):
+
+
+def place_kernel(devices, shift, pattern_ref, source_ref, far_ref, back_ref):
     cam_dev = pattern_ref.shape[1]
     count = jnp.zeros((devices, cam_dev), F32)
     sources = []
@@ -163,12 +188,17 @@
         withins.append(iota((cam_dev, cam_dev), 0) == within)
         count = count + dot_nt(one_hot(sources[k]), one_hot(withins[k]))
         source_ref[:, k * cam_dev : (k + 1) * cam_dev] = source.astype(F32)
-    rank = dot_nn(one_hot(count > 0), before(cam_dev))
+    found = one_hot(count > 0)
+    rank = dot_nn(found, before(cam_dev))
+    most = jnp.sum(found.astype(F32), axis=1, keepdims=True)
     turned = rank.T.astype(BF16)
     for k in range(NBR):
         column = dot_nn(turned, one_hot(sources[k]))
         mine = jnp.sum(jnp.where(withins[k], column, 0.0), axis=0, keepdims=True)
         far_ref[:, k * cam_dev : (k + 1) * cam_dev] = mine
+        full = jnp.sum(jnp.where(sources[k], most, 0.0), axis=0, keepdims=True)
+        back = SLOTS - 1.0 - mine
+        back_ref[:, k * cam_dev : (k + 1) * cam_dev] = jnp.where(back >= full, back, -1.0)
 
 
 def outer(left, right, extra):
@@ -202,7 +232,7 @@
 
 
 def diagonal_kernel(
-    got_ref, rank_ref, text_ref, out_ref, lower_ref, state_ref, send_ref
+    got_ref, rank_ref, back_ref, text_ref, out_ref, lower_ref, state_ref, send_ref
 ):
     devices = got_ref.shape[0] // 10
     cam_dev = out_ref.shape[1]
@@ -237,11 +267,13 @@
     for index in range(4, 7):
         state_ref[index] = zero
     most = jnp.max(jnp.max(rank_ref[...], axis=1, keepdims=True), axis=0, keepdims=True)
-    crowded = jnp.where(most >= float(GROUP * ROWS), 1.0, 0.0)
-    send_rows(send_ref, scaled, GROUP, ranked(rank_ref), ROWS, [crowded])
-
-
-def coupling_kernel(text_ref, out_ref, wanted_ref):
+    single = jnp.logical_and(rank_ref[...] >= 0, back_ref[...] < 0)
+    carried = total_of(jnp.where(single, 1.0, 0.0))
+    crowded = jnp.where(jnp.logical_or(most >= float(SLOTS), carried > float(CARRIED)), 1.0, 0.0)
+    send_rows(send_ref, [coupled(scaled, rank_ref)], ROWS, [crowded])
+
+
+def coupling_kernel(text_ref, lower_ref, out_ref, wanted_ref, inverse_ref):
     cam_dev = out_ref.shape[2]
     devices = wanted_ref.shape[0]
     out_ref[...] = jnp.zeros_like(out_ref)
@@ -261,12 +293,20 @@
         return 0
 
     lax.fori_loop(0, OBS_CAP // 2, step, 0)
-    lines = []
+    labels = []
     for s in range(OBS_CAP):
         label = text_ref[s // 2, 77:78, (s % 2) * devices : (s % 2 + 1) * devices]
-        lines.append(label - cam_dev * quotient(label, cam_dev))
-    lines.append(jnp.zeros((128 - OBS_CAP, devices), F32))
-    wanted_ref[...] = jnp.concatenate(lines, axis=0).T
+        labels.append(label - cam_dev * quotient(label, cam_dev))
+    labels.append(jnp.zeros((128 - OBS_CAP, devices), F32))
+    wanted_ref[...] = jnp.concatenate(labels, axis=0).T
+    row = iota((16, 9 * cam_dev), 0)
+    unit = lax.shift_right_logical(iota((16, 9 * cam_dev), 1), cam_dev.bit_length() - 1) == row
+    solved = solve(lower_ref, jnp.where(unit, 1.0, 0.0))
+    columns = [solved[:, c * cam_dev : (c + 1) * cam_dev] for c in range(9)]
+    inverse_ref[...] = jnp.concatenate(
+        [column[:8] for column in columns] + [columns[8][:8], columns[8][8:], jnp.zeros((8, cam_dev), F32)],
+        axis=0,
+    )
 
 
 def cholesky(cells_ref, lower_ref):
@@ -310,117 +350,135 @@
     return rest
 
 
-def multiply(cells_ref, diagonal_ref, taken, own):
-    cam_dev = own.shape[1]
+def multiply(pairs):
+    cam_dev = pairs[0][1].shape[1]
     sums = [jnp.zeros((8, cam_dev), F32) for _ in range(9)]
     side = jnp.zeros((8, cam_dev), F32)
     corner = jnp.zeros((1, cam_dev), F32)
-    for k in range(NBR + 1):
-        vector = own if k == NBR else taken[:, k * cam_dev : (k + 1) * cam_dev]
+    for cell_ref, vector in pairs:
         first, last = vector[0:8], vector[8:9]
-        cell_ref = diagonal_ref if k == NBR else cells_ref.at[k]
         for r in range(9):
             sums[r] = sums[r] + cell_ref[8 * r : 8 * r + 8, :] * first
         side = side + cell_ref[72:80, :] * last
         corner = corner + cell_ref[80:81, :] * last
-    lines = [jnp.sum(part, axis=0, keepdims=True) for part in sums]
-    top = jnp.concatenate(lines[:8], axis=0) + side
-    return jnp.concatenate([top, lines[8] + corner, jnp.zeros((7, cam_dev), F32)], axis=0)
+    sums = [jnp.sum(part, axis=0, keepdims=True) for part in sums]
+    top = jnp.concatenate(sums[:8], axis=0) + side
+    return jnp.concatenate([top, sums[8] + corner, jnp.zeros((7, cam_dev), F32)], axis=0)
 
 
 def total_of(values):
     return jnp.sum(jnp.sum(values, axis=1, keepdims=True), axis=0, keepdims=True)
 
 
-def spread(vector, row_of):
+def lane_plan():
+    lane = iota((128, 1), 0)
+    group = jnp.where(lane < 112, lax.shift_right_logical(lane, 3), lane - 112)
+    return group, jnp.where(lane < 112, lane & 7, 8)
+
+
+def spread(vector):
     cam_dev = vector.shape[1]
-    choose = one_hot(iota((128, vector.shape[0]), 1).astype(F32) == row_of)
+    choose = one_hot(iota((128, 16), 1) == lane_plan()[1])
     copies = dot_nn(choose, jnp.concatenate(pieces(vector), axis=1))
     return [copies[:, p * cam_dev : (p + 1) * cam_dev] for p in range(3)]
 
 
-def lane_groups(count):
-    size = 126 // count
-    lane = iota((128, 1), 0)
-    group = quotient(lane, size)
-    return group, lane.astype(F32) - group * size
-
-
-def value_rows(count, values):
-    if count == PAIRS:
-        return jnp.where(values < 9, values, values + 7)
-    return values
-
-
-def ranked(rank_ref):
+def coupled(vector, rank_ref):
+    group, _ = lane_plan()
     rank = rank_ref[...]
-    return lambda slot: one_hot(rank == float(slot))
-
-
-def send_rows(send_ref, vector, count, hits_of, rows, scalars):
+    copies = spread(vector)
+    right = [
+        jnp.concatenate([jnp.where(group == g, part, 0.0) for g in range(GROUP)], axis=1) for part in copies
+    ]
+    left = [[one_hot(rank == float(GROUP * h + g)) for g in range(GROUP)] for h in range(ROWS)]
+    return left, right
+
+
+def observed(first, second, wanted_ref):
+    group, _ = lane_plan()
+    lane = iota((wanted_ref.shape[0], first.shape[1]), 1).astype(F32)
+    right = [
+        jnp.concatenate(
+            [
+                jnp.where(group == 2 * g, one, jnp.where(group == 2 * g + 1, two, 0.0))
+                for g in range(PAIRS)
+            ],
+            axis=1,
+        )
+        for one, two in zip(spread(first), spread(second))
+    ]
+    empty = jnp.zeros(lane.shape, BF16)
+    left = [
+        [
+            one_hot(wanted_ref[:, slot : slot + 1] == lane) if slot < OBS_CAP else empty
+            for slot in range(PAIRS * h, PAIRS * h + PAIRS)
+        ]
+        for h in range(PAIR_ROWS)
+    ]
+    return left, right
+
+
+def send_rows(send_ref, parts, rows, scalars):
     devices = send_ref.shape[0] // rows
-    group, value = lane_groups(count)
-    copies = spread(vector, value_rows(count, value))
+    left = jnp.concatenate(
+        [jnp.concatenate([hit for part in parts for hit in part[0][h]], axis=1) for h in range(rows)], axis=0
+    )
     right = jnp.concatenate(
-        [
-            jnp.concatenate([jnp.where(group == float(g), part, 0.0) for g in range(count)], axis=1)
-            for part in copies
-        ],
-        axis=0,
+        [jnp.concatenate([part[1][p] for part in parts], axis=1) for p in range(3)], axis=0
     ).astype(BF16)
+    sums = dot_nt(left, right)
     lane = iota((devices, 128), 1)
     for h in range(rows):
-        hits = [hits_of(count * h + g) for g in range(count)]
-        sums = dot_nt(jnp.concatenate(hits, axis=1), right)
-        text = sums[:, :128] + sums[:, 128:256] + sums[:, 256:]
+        mine = sums[h * devices : (h + 1) * devices]
+        text = mine[:, :128] + mine[:, 128:256] + mine[:, 256:]
         for index, scalar in enumerate(scalars[2 * h : 2 * h + 2]):
             text = jnp.where(lane == 126 + index, scalar, text)
         send_ref[pl.ds(h, devices, stride=rows), :] = text
 
 
-def read_rows(got, rows, count, places, groups, height, scalars):
-    turned = got.T
-    total = turned.shape[1]
-    group, _ = lane_groups(count)
-    mark = one_hot(iota((total, places.shape[1]), 0).astype(F32) == places)
+def read_rows(turned, places):
+    mark = one_hot(iota((turned.shape[1], places.shape[1]), 0).astype(F32) == places)
     taken = dot_nn(jnp.concatenate(pieces(turned), axis=0), mark)
-    group = jnp.concatenate([group] * 3, axis=0)
-    kept = jnp.where(group == groups, taken, 0.0).astype(BF16)
-    lane = iota((height, 128), 1)
-    size = 126 // count
-    value = value_rows(count, lane.astype(F32) - quotient(lane, size) * size)
-    fold = one_hot(jnp.logical_and(iota((height, 128), 0).astype(F32) == value, lane < 126))
-    vectors = dot_nn(jnp.concatenate([fold] * 3, axis=1), kept)
-    column = iota((1, total), 1)
+    return taken[:128] + taken[128:256] + taken[256:]
+
+
+def pick(taken, groups):
+    top = jnp.zeros((8, taken.shape[1]), F32)
+    for g in range(GROUP):
+        top = jnp.where(groups == float(g), taken[8 * g : 8 * g + 8], top)
+    ninth = jnp.where(iota((16, taken.shape[1]), 0).astype(F32) == groups, taken[112:128], 0.0)
+    ninth = jnp.sum(ninth, axis=0, keepdims=True)
+    return jnp.concatenate([top, ninth, jnp.zeros((7, taken.shape[1]), F32)], axis=0)
+
+
+def read_scalars(turned, rows, count):
+    column = iota((1, turned.shape[1]), 1)
     inner = column.astype(F32) - quotient(column, rows) * rows
     sums = []
-    for index in range(scalars):
+    for index in range(count):
         line = turned[126 + index % 2 : 127 + index % 2]
         sums.append(
             jnp.sum(jnp.where(inner == float(index // 2), line, 0.0), axis=1, keepdims=True)
         )
-    return vectors, sums
-
-
-def wide(index):
-    return index >= 2
-
-
-def layout(index):
-    return (2 * ROWS, PAIRS) if wide(index) else (ROWS, GROUP)
+    return sums
 
 
 def step_kernel(
-    index, got_ref, source_ref, place_ref, rank_ref, cells_ref, diagonal_ref, lower_ref, state_ref, far_ref,
-    state_out, far_out, send_ref,
+    index, got_ref, source_ref, place_ref, second_ref, rank_ref, back_ref, cells_ref, diagonal_ref, inverse_ref,
+    state_ref, far_ref, state_out, far_out, send_ref,
 ):
-    rows, count = layout(index)
-    part = quotient(place_ref[...], count)
-    places, groups = source_ref[...] * rows + part, place_ref[...] - part * count
-    arrived, sums = read_rows(
-        got_ref[...], rows, count, places, groups, 32 if wide(index) else 16, 4 if index else 1
-    )
-    cam_dev = cells_ref.shape[2]
+    turned = got_ref[...].T
+    sums = read_scalars(turned, ROWS, 4 if index else 1)
+    source = source_ref[...]
+    part = quotient(place_ref[...], GROUP)
+    places, groups = source * ROWS + part, place_ref[...] - part * GROUP
+    couplings = places.shape[1]
+    if index >= 2:
+        part = quotient(jnp.maximum(second_ref[...], 0.0), GROUP)
+        room = second_ref[...] >= 0
+        places = jnp.concatenate([places, jnp.where(room, source * ROWS + part, -1.0)], axis=1)
+        groups = jnp.concatenate([groups, second_ref[...] - part * GROUP], axis=1)
+    arrived = pick(read_rows(turned, places), groups)
     step, rest, scaled, direction = (state_ref[i] for i in range(4))
     if index:
         image, image_scaled = state_ref[4], state_ref[5]
@@ -430,42 +488,41 @@
         step = step + alpha * direction
         rest = rest - alpha * image
         direction = (scaled - alpha * image_scaled) + beta * direction
-        far_before = arrived[16:] if wide(index) else far_ref[...]
-        far = (far_before - alpha * arrived[:16]) + beta * far_ref[...]
+        far_before = far_ref[1]
+        if index >= 2:
+            far_before = jnp.where(room, arrived[:, couplings:], far_before)
+        far_scaled = far_before - alpha * arrived[:, :couplings]
+        far = far_scaled + beta * far_ref[0]
     else:
+        far_scaled = arrived
         far = arrived
-    image = multiply(cells_ref, diagonal_ref, far, direction)
+    cam_dev = cells_ref.shape[2]
+    image = multiply(
+        [(diagonal_ref, direction)]
+        + [(cells_ref.at[k], far[:, k * cam_dev : (k + 1) * cam_dev]) for k in range(NBR)]
+    )
     energy = total_of(direction * image)
+    scaled = multiply([(inverse_ref, rest)]) if index else scaled
+    old = total_of(rest * scaled)
     state_out[0] = step
     state_out[1] = rest
+    state_out[2] = scaled
     state_out[3] = direction
     state_out[4] = image
     state_out[6] = state_ref[6] if index else jnp.zeros_like(step) + sums[0]
-    far_out[...] = far
+    far_out[0] = far
+    far_out[1] = far_scaled
     if index == ITERS - 1:
-        scaled = solve(lower_ref, rest)
-        state_out[2] = scaled
         state_out[5] = jnp.zeros_like(image)
-        lane = iota((rank_ref.shape[0], cam_dev), 1).astype(F32)
-
-        def wanted(slot):
-            if slot < OBS_CAP:
-                return one_hot(rank_ref[:, slot : slot + 1] == lane)
-            return jnp.zeros(lane.shape, BF16)
-
-        both = jnp.concatenate([step, direction], axis=0)
-        send_rows(send_ref, both, PAIRS, wanted, PAIR_ROWS, [energy, total_of(rest * scaled)])
+        send_rows(send_ref, [observed(step, direction, rank_ref)], PAIR_ROWS, [energy, old])
         return
-    solved = solve(lower_ref, jnp.concatenate([rest, image], axis=1))
-    scaled, image_scaled = solved[:, :cam_dev], solved[:, cam_dev:]
-    state_out[2] = scaled
+    image_scaled = multiply([(inverse_ref, image)])
     state_out[5] = image_scaled
-    scalars = [
-        energy, total_of(scaled * image), total_of(image * image_scaled), total_of(rest * scaled)
-    ]
-    rows, count = layout(index + 1)
-    vector = jnp.concatenate([image_scaled, scaled], axis=0) if wide(index + 1) else image_scaled
-    send_rows(send_ref, vector, count, ranked(rank_ref), rows, scalars)
+    parts = [coupled(image_scaled, rank_ref)]
+    if index + 1 >= 2:
+        parts.append(coupled(scaled, back_ref))
+    scalars = [energy, total_of(scaled * image), total_of(image * image_scaled), old]
+    send_rows(send_ref, parts, ROWS, scalars)
 
 
 def finish_kernel(
@@ -474,20 +531,24 @@
     npts = used_ref.shape[1]
     places = jnp.concatenate([place_ref[a : a + 1, :] for a in range(TRACK)], axis=1)
     groups = jnp.concatenate([place_ref[TRACK + a : TRACK + a + 1, :] for a in range(TRACK)], axis=1)
-    seen, sums = read_rows(got_ref[...], PAIR_ROWS, PAIRS, places, groups, 32, 2)
-    alpha = sums[1] / sums[0]
+    turned = got_ref[...].T
+    energy, old = read_scalars(turned, PAIR_ROWS, 2)
+    alpha = old / energy
     step_ref[...] = (state_ref[0] + alpha * state_ref[3])[:9]
     rest_ref[...] = (state_ref[1] - alpha * state_ref[4])[:9]
-    moved = seen[:16] + alpha * seen[16:]
+    taken = read_rows(turned, places)
+    moved = pick(taken, 2.0 * groups) + alpha * pick(taken, 2.0 * groups + 1.0)
     reduced = [jnp.zeros((1, npts), F32) for _ in range(3)]
     for a in range(TRACK):
         live = used_ref[a : a + 1, :].astype(F32)
         there = moved[:9, a * npts : (a + 1) * npts]
+        jacobian = lines(jc_ref, a, 0, 18, npts)
+        gradient = lines(jp_ref, a, 0, 6, npts)
         for u in range(2):
-            change = jnp.sum(jc_ref[9 * u : 9 * u + 9, a, :] * there, axis=0, keepdims=True)
+            change = jnp.sum(jacobian[9 * u : 9 * u + 9] * there, axis=0, keepdims=True)
             change = live * (change + rs_ref[a, u : u + 1, :])
             for x in range(3):
-                reduced[x] = reduced[x] - jp_ref[3 * u + x : 3 * u + x + 1, a, :] * change
+                reduced[x] = reduced[x] - gradient[3 * u + x : 3 * u + x + 1] * change
     for x in range(3):
         point_ref[x : x + 1, :] = sum(
             vi_ref[3 * x + y : 3 * x + y + 1, :] * reduced[y] for y in range(3)
@@ -595,19 +656,21 @@
     shift = cam_dev.bit_length() - 1
     couplings = NBR * cam_dev
 
-    cameras = jnp.transpose(jacobian_cam, (1, 0, 2))
-    points = jnp.transpose(jacobian_pt, (1, 0, 2))
-
-    packed, places, rank = call(
+    cameras = flat(jacobian_cam)
+    points = flat(jacobian_pt)
+
+    packed, places, rank, back = call(
         functools.partial(pack_kernel, devices, shift),
-        (shape(devices * 10, 128), shape(2 * TRACK, npts), shape(devices, cam_dev)),
+        (
+            shape(devices * 10, 128), shape(2 * TRACK, npts), shape(devices, cam_dev), shape(devices, cam_dev),
+        ),
         "pack",
         [pltpu.VMEM((80, TRACK * npts), F32)],
     )(cameras, points, residuals, point_inverse, obs_camera, pair_slot, observation_used, pattern)
     got = exchange(packed, devices)
-    sources, far_rank = call(
+    sources, far_rank, far_back = call(
         functools.partial(place_kernel, devices, shift),
-        (shape(1, couplings), shape(1, couplings)),
+        (shape(1, couplings), shape(1, couplings), shape(1, couplings)),
         "place",
         flops=4 * 10**9,
     )(pattern)
@@ -621,25 +684,26 @@
             shape(devices * ROWS, 128),
         ),
         "diagonal",
-    )(got, rank)
-    cells, wanted = call(
+    )(got, rank, back)
+    cells, wanted, inverse = call(
         coupling_kernel,
-        (shape(NBR, CELL, cam_dev), shape(devices, 128)),
+        (shape(NBR, CELL, cam_dev), shape(devices, 128), shape(CELL, cam_dev)),
         "coupling",
         flops=8 * 10**9,
-    )(text)
-    far = jnp.zeros((16, couplings), F32)
+    )(text, lower)
+    far = jnp.zeros((2, 16, couplings), F32)
     crowded = None
     for index in range(ITERS):
         last = index == ITERS - 1
-        rows = PAIR_ROWS if last else layout(index + 1)[0]
+        rows = PAIR_ROWS if last else ROWS
         arrived = exchange(message, devices)
         state, far, message = call(
             functools.partial(step_kernel, index),
-            (shape(7, 16, cam_dev), shape(16, couplings), shape(devices * rows, 128)),
+            (shape(7, 16, cam_dev), shape(2, 16, couplings), shape(devices * rows, 128)),
             "step",
         )(
-            arrived, sources, far_rank, wanted if last else rank, cells, diagonal, lower, state, far
+            arrived, sources, far_rank, far_back, wanted if last else rank, back, cells, diagonal, inverse,
+            state, far,
         )
         if index == 0:
             crowded = state[6, 0, 0] > 0.0

time: 230 us -> 220 us (0.957)
  blocking collectives: 88.1 us -> 78.9 us
    all_to_all x3, blocking collectives: 88.1 us -> 78.9 us  [exchange(): lax.all_to_all(message.reshape(devices, width, 1, 128), BOTH, split_axis=...]
  transfers between devices with their start and end apart: 3 -> 3, of which waited for: 3 -> 3; matrix products, arithmetic and copies ran while one was open for 0% -> 0% of each run, Pallas kernels for 5% -> 6%
where the time goes in v3:
time: 220 us; the launch traced here: 218 us
  blocking collectives  78.9 us (36%)
  waiting for transfers between devices  55.1 us (25%)
  Pallas kernels  37.8 us (17%)
  starting transfers between devices  28.6 us (13%)
  between operations  15 us (7%)
  local copies, waits for them, and re-layouts  2.52 us (1%)
    all_to_all x3, blocking collectives, exchange(): lax.all_to_all(message.reshape(devices, width, 1, 128), BOTH, split_axis=...  78.9 us
    all_to_all x3, waiting for transfers between devices, exchange(): lax.all_to_all(message.reshape(devices, width, 1, 128), BOTH, split_axis=...  55.1 us
    all_to_all x3, starting transfers between devices, exchange(): lax.all_to_all(message.reshape(devices, width, 1, 128), BOTH, split_axis=...  28.6 us
    pallas_call x4, Pallas kernels, per_device(): call(functools.partial(step_kernel, index), (shape(7, 16, cam_dev), shape...  12.3 us
    pallas_call x1, Pallas kernels, per_device(): call(coupling_kernel, (shape(NBR, CELL, cam_dev), shape(devices, 128), sh...  10 us
    pallas_call x1, Pallas kernels, per_device(): call(functools.partial(pack_kernel, devices, shift), (shape(devices * 10,...  7.47 us
  transfers between devices with their start and end apart: 3, of which 3 were waited for; matrix products, arithmetic and copies ran while one was open for 0% of the time, Pallas kernels for 6%

profile of v3, /device:TPU:1, one launch (start us, length us, event | category | flops | bytes accessed | tf_op | source)
XLA Modules:
  0.0 218.0 jit_solution(9847003945023875259)
XLA Ops:
  7.2 0.0 copy-start
  7.2 0.7 copy-done
  7.9 7.5 %pack.1 = (f32[2560,128]{1,0:T(8,128)}, f32[8,512]{1,0:T(8,128)S(1)}, f32[256,128]{1,0:T(8,128)S(1)}, f32[256,128]{1,0:T(8,128)S(1)}) custom-call(f32[288,128]{1,0:T(8,128)} %bitcast.632, f32[96,128]{1,0:T(8,128)} %bitcast.640, f32[4,2,512]{2,1,0:T(2,128)} %rs_ref.3, f32[9,512]{1,0:T(8,128)} %vi_ref.3, s32[4,512]{1,0:T(4,128)} %cam_ref.1, ...), custom_call_target="tpu_custom_call" | custom-call | tf_op jit(solution)/shard_map/pack/pallas_call | solution.py:662
  15.4 15.7 %all-to-all-start = ((f32[256,10,1,128]{3,2,1,0:T(1,128)}), f32[256,10,1,128]{3,2,1,0:T(1,128)S(1)}, u32[]{:S(2)}, u32[]{:S(2)}) async-start(f32[256,10,1,128]{3,2,1,0:T(1,128)} %bitcast.117), calls=%async_computation | async-start | bytes 2621440 | tf_op jit(solution)/shard_map/all_to_all | solution.py:644
  31.1 2.0 place.1
  33.1 34.0 %all-to-all-done = f32[256,10,1,128]{3,2,1,0:T(1,128)S(1)} async-done(((f32[256,10,1,128]{3,2,1,0:T(1,128)}), f32[256,10,1,128]{3,2,1,0:T(1,128)S(1)}, u32[]{:S(2)}, u32[]{:S(2)}) %all-to-all-start) | async-done | bytes 1310752 | tf_op jit(solution)/shard_map/all_to_all | solution.py:644
  67.1 4.3 %diagonal.1 = (f32[8,80,512]{2,1,0:T(8,128)S(1)}, f32[96,128]{1,0:T(8,128)}, f32[9,16,128]{2,1,0:T(8,128)S(1)}, f32[7,16,128]{2,1,0:T(8,128)S(1)}, f32[512,128]{1,0:T(8,128)}) custom-call(f32[2560,128]{1,0:T(8,128)S(1)} %bitcast.609, f32[256,128]{1,0:T(8,128)S(1)} %get-tuple-element.63.rank_ref, f32[256,128]{1,0:T(8,128)S(1)} %get-tuple-element.64.back_ref), custom_call_target="tpu_custom_call" | custom-call | tf_op jit(solution)/shard_map/diagonal/pallas_call | solution.py:677
  71.3 0.0 copy-start.1
  71.3 7.1 %all-to-all-start.1 = ((f32[256,2,1,128]{3,1,2,0:T(2,128)}), f32[256,2,1,128]{3,1,2,0:T(2,128)S(1)}, u32[]{:S(2)}, u32[]{:S(2)}) async-start(f32[256,2,1,128]{3,1,2,0:T(2,128)} %bitcast.120), calls=%async_computation.1 | async-start | bytes 524288 | tf_op jit(solution)/shard_map/all_to_all | solution.py:644
  78.4 0.0 copy-start.2
  78.5 0.0 copy-start.3
  78.5 0.0 copy-start.4
  78.5 0.0 copy-start.8
  78.5 0.0 copy-start.10
  78.5 0.0 copy-start.11
  78.5 0.0 copy-start.12
  78.5 10.0 %coupling.1 = (f32[12,96,128]{2,1,0:T(8,128)S(1)}, f32[256,128]{1,0:T(8,128)S(1)}, f32[96,128]{1,0:T(8,128)S(1)}) custom-call(f32[8,80,512]{2,1,0:T(8,128)S(1)} %get-tuple-element.69.text_ref, f32[9,16,128]{2,1,0:T(8,128)S(1)} %get-tuple-element.70.lower_ref), custom_call_target="tpu_custom_call" | custom-call | flops 8000000000 | bytes 1048576 | tf_op jit(solution)/shard_map/coupling/pallas_call | solution.py:688
  88.6 5.1 %all-to-all-done.1 = f32[256,2,1,128]{3,1,2,0:T(2,128)S(1)} async-done(((f32[256,2,1,128]{3,1,2,0:T(2,128)}), f32[256,2,1,128]{3,1,2,0:T(2,128)S(1)}, u32[]{:S(2)}, u32[]{:S(2)}) %all-to-all-start.1) | async-done | bytes 262176 | tf_op jit(solution)/shard_map/all_to_all | solution.py:644
  93.7 0.0 copy-done.1
  93.7 2.1 step.4
  95.8 23.8 %all_to_all.30 = f32[256,2,1,128]{3,1,2,0:T(2,128)S(1)} all-to-all(f32[256,2,1,128]{3,1,2,0:T(2,128)S(1)} %bitcast.616), channel_id=1, replica_groups=mesh['cam'=32,'pt'=8] {'cam','pt'}, dimensions={0} | all-to-all | bytes 524288 | tf_op jit(solution)/shard_map/all_to_all | solution.py:644
  119.6 3.1 %step.5 = (f32[7,16,128]{2,1,0:T(8,128)S(1)}, f32[2,16,1536]{2,1,0:T(8,128)S(1)}, f32[512,128]{1,0:T(8,128)S(1)}) custom-call(f32[512,128]{1,0:T(8,128)S(1)} %bitcast.614, f32[1,1536]{1,0:T(1,128)S(1)} %get-tuple-element.66.source_ref, f32[1,1536]{1,0:T(1,128)S(1)} %get-tuple-element.67.place_ref, f32[1,1536]{1,0:T(1,128)S(1)} %get-tuple-element.68.second_ref, ...), custom_call_target="tpu_custom_call" | custom-call | tf_op jit(solution)/shard_map/step/pallas_call | solution.py:700
  122.7 20.9 %all_to_all.31 = f32[256,2,1,128]{3,1,2,0:T(2,128)S(1)} all-to-all(f32[256,2,1,128]{3,1,2,0:T(2,128)S(1)} %bitcast.617), channel_id=1, replica_groups=mesh['cam'=32,'pt'=8] {'cam','pt'}, dimensions={0} | all-to-all | bytes 524288 | tf_op jit(solution)/shard_map/all_to_all | solution.py:644
  143.7 3.8 %step.6 = (f32[7,16,128]{2,1,0:T(8,128)S(1)}, f32[2,16,1536]{2,1,0:T(8,128)S(1)}, f32[512,128]{1,0:T(8,128)S(1)}) custom-call(f32[512,128]{1,0:T(8,128)S(1)} %bitcast.613, f32[1,1536]{1,0:T(1,128)S(1)} %get-tuple-element.66.source_ref, f32[1,1536]{1,0:T(1,128)S(1)} %get-tuple-element.67.place_ref, f32[1,1536]{1,0:T(1,128)S(1)} %get-tuple-element.68.second_ref, ...), custom_call_target="tpu_custom_call" | custom-call | tf_op jit(solution)/shard_map/step/pallas_call | solution.py:700
  147.4 34.2 %all_to_all.32 = f32[256,2,1,128]{3,1,2,0:T(2,128)S(1)} all-to-all(f32[256,2,1,128]{3,1,2,0:T(2,128)S(1)} %bitcast.615), channel_id=1, replica_groups=mesh['cam'=32,'pt'=8] {'cam','pt'}, dimensions={0} | all-to-all | bytes 524288 | tf_op jit(solution)/shard_map/all_to_all | solution.py:644
  181.6 3.3 %step.7 = (f32[7,16,128]{2,1,0:T(8,128)S(1)}, f32[2,16,1536]{2,1,0:T(8,128)}, f32[768,128]{1,0:T(8,128)}) custom-call(f32[512,128]{1,0:T(8,128)S(1)} %bitcast.612, f32[1,1536]{1,0:T(1,128)S(1)} %get-tuple-element.66.source_ref, f32[1,1536]{1,0:T(1,128)S(1)} %get-tuple-element.67.place_ref, f32[1,1536]{1,0:T(1,128)S(1)} %get-tuple-element.68.second_ref, ...), custom_call_target="tpu_custom_call" | custom-call | tf_op jit(solution)/shard_map/step/pallas_call | solution.py:700
  184.9 5.9 %all-to-all-start.5 = ((f32[256,3,1,128]{3,2,1,0:T(1,128)}), f32[256,3,1,128]{3,2,1,0:T(1,128)S(1)}, u32[]{:S(2)}, u32[]{:S(2)}) async-start(f32[256,3,1,128]{3,2,1,0:T(1,128)} %bitcast.132), calls=%async_computation.5 | async-start | bytes 786432 | tf_op jit(solution)/shard_map/all_to_all | solution.py:644
  190.8 0.5 slice.280
  192.0 16.1 %all-to-all-done.5 = f32[256,3,1,128]{3,2,1,0:T(1,128)S(1)} async-done(((f32[256,3,1,128]{3,2,1,0:T(1,128)}), f32[256,3,1,128]{3,2,1,0:T(1,128)S(1)}, u32[]{:S(2)}, u32[]{:S(2)}) %all-to-all-start.5) | async-done | bytes 393248 | tf_op jit(solution)/shard_map/all_to_all | solution.py:644
  208.0 0.0 copy-done.2
  208.0 0.0 copy-done.3
  208.0 0.0 copy-done.4
  208.0 0.0 copy-done.8
  208.0 0.0 copy-done.10
  208.0 1.7 finish.1
  209.8 0.0 copy-done.11
  209.8 0.0 copy-done.12
  209.8 0.0 copy-start.13
  209.8 0.6 copy-done.13
  210.4 0.0 copy-start.14
  210.4 0.6 copy-done.14
  (2 shorter events, 0.0 us)
Async XLA Ops:
  7.2 0.8 copy-start
  15.4 51.7 %all-to-all-start = ((f32[256,10,1,128]{3,2,1,0:T(1,128)}), f32[256,10,1,128]{3,2,1,0:T(1,128)S(1)}, u32[]{:S(2)}, u32[]{:S(2)}) async-start(f32[256,10,1,128]{3,2,1,0:T(1,128)} %bitcast.117), calls=%async_computation | async-start | bytes 2621440 | tf_op jit(solution)/shard_map/all_to_all | solution.py:644
  71.3 22.3 %copy-start.1 = (f32[96,128]{1,0:T(8,128)S(1)}, f32[96,128]{1,0:T(8,128)}, u32[]{:S(2)}) copy-start(f32[96,128]{1,0:T(8,128)} %get-tuple-element.72.diagonal_ref) | copy-start | bytes 147460
  71.3 22.3 %all-to-all-start.1 = ((f32[256,2,1,128]{3,1,2,0:T(2,128)}), f32[256,2,1,128]{3,1,2,0:T(2,128)S(1)}, u32[]{:S(2)}, u32[]{:S(2)}) async-start(f32[256,2,1,128]{3,1,2,0:T(2,128)} %bitcast.120), calls=%async_computation.1 | async-start | bytes 524288 | tf_op jit(solution)/shard_map/all_to_all | solution.py:644
  78.4 129.6 %copy-start.2 = (f32[4,18,512]{2,0,1:T(4,128)S(1)}, f32[4,18,512]{2,0,1:T(4,128)}, u32[]{:S(2)}) copy-start(f32[4,18,512]{2,0,1:T(4,128)} %param.10) | copy-start | bytes 442372
  78.5 129.6 %copy-start.3 = (f32[4,6,512]{2,0,1:T(4,128)S(1)}, f32[4,6,512]{2,0,1:T(4,128)}, u32[]{:S(2)}) copy-start(f32[4,6,512]{2,0,1:T(4,128)} %param.11) | copy-start | bytes 147460
  78.5 129.5 %copy-start.4 = (f32[9,512]{1,0:T(8,128)S(1)}, f32[9,512]{1,0:T(8,128)}, u32[]{:S(2)}) copy-start(f32[9,512]{1,0:T(8,128)} %vi_ref.3) | copy-start | bytes 55300
  78.5 129.5 %copy-start.8 = (f32[4,2,512]{2,1,0:T(2,128)S(1)}, f32[4,2,512]{2,1,0:T(2,128)}, u32[]{:S(2)}) copy-start(f32[4,2,512]{2,1,0:T(2,128)} %rs_ref.3) | copy-start | bytes 49156
  78.5 129.5 %copy-start.10 = (s32[4,512]{1,0:T(4,128)S(1)}, s32[4,512]{1,0:T(4,128)}, u32[]{:S(2)}) copy-start(s32[4,512]{1,0:T(4,128)} %used_ref.3) | copy-start | bytes 24580
  78.5 131.3 %copy-start.11 = (s32[4,512]{1,0:T(4,128)S(1)}, s32[4,512]{1,0:T(4,128)}, u32[]{:S(2)}) copy-start(s32[4,512]{1,0:T(4,128)} %cam_ref.1) | copy-start | bytes 24580
  78.5 131.3 %copy-start.12 = (s32[12,128]{1,0:T(8,128)S(1)}, s32[12,128]{1,0:T(8,128)}, u32[]{:S(2)}) copy-start(s32[12,128]{1,0:T(8,128)} %pattern_ref.3) | copy-start | bytes 18436
  184.9 23.1 %all-to-all-start.5 = ((f32[256,3,1,128]{3,2,1,0:T(1,128)}), f32[256,3,1,128]{3,2,1,0:T(1,128)S(1)}, u32[]{:S(2)}, u32[]{:S(2)}) async-start(f32[256,3,1,128]{3,2,1,0:T(1,128)} %bitcast.132), calls=%async_computation.5 | async-start | bytes 786432 | tf_op jit(solution)/shard_map/all_to_all | solution.py:644
  209.8 0.6 copy-start.13
  210.4 0.6 copy-start.14
